TPU v7x, 32 devices: a whole 2x2x4 slice. The times are simulated.
32 devices in a mesh: dp: 2 (over y), ctx: 16 (over z, x, core).
Axes of the slice: x: 2, y: 2, z: 4, core: 2. Of those that a mesh axis runs over, the one named last changes fastest.
Arguments:
- queries: bfloat16 [2, 2048, 1024], P('dp', 'ctx'), may hold values from -6 to 6
- keys: bfloat16 [2, 2048, 1024], P('dp', 'ctx'), may hold values from -6 to 6
- values: bfloat16 [2, 2048, 1024], P('dp', 'ctx'), may hold values from -6 to 6
- rel_bias: float32 [16, 769], replicated, may hold values from -8 to 8
- grad_out: bfloat16 [2, 2048, 1024], P('dp', 'ctx'), may hold values from -6 to 6
Outputs:
- attended: bfloat16 [2, 2048, 1024], P('dp', 'ctx')
- grad_queries: bfloat16 [2, 2048, 1024], P('dp', 'ctx')
- grad_keys: bfloat16 [2, 2048, 1024], P('dp', 'ctx')
- grad_values: bfloat16 [2, 2048, 1024], P('dp', 'ctx')
- grad_bias: float32 [16, 769], replicated
All inputs are finite; a program needn't handle non-finite values.
Results may differ from a plain program's by a relative error of at most 0.024.
Values may be sent and summed in bfloat16 or wider, within the bound.
A program may use at most 128 MiB of HBM per device.

v0:
```python
import functools
import math

import jax
import jax.numpy as jnp
from jax import lax
from jax.experimental import pallas as pl
from jax.experimental.pallas import tpu as pltpu
from jax.sharding import PartitionSpec as P

HEADS = 16
HEAD = 64
NB = 3
GROUP = 4
PAIRS = HEADS // GROUP // 2
LANES = 2 * HEAD
EXCLUDED = -1e30
MESH = pl.DeviceIdType.MESH
Q, K, V, G = 0, 1, 2, 3
NT = (((1,), (1,)), ((), ()))
TN = (((0,), (0,)), ((), ()))


def dot(a, b, dims=(((1,), (0,)), ((), ()))):
    return lax.dot_general(a, b, dims, preferred_element_type=jnp.float32)


def kernel(
    n_dp, n_groups, frames,
    q_hbm, k_hbm, v_hbm, g_hbm, rev_ref,
    att_out, gq_out, gk_out, gv_out, bias_out,
    qbuf, gbuf, kbuf, vbuf, bias_tab, bias_acc, gk_acc, gv_acc,
    halo_out, halo_in, ostage, b1buf, b2buf, sum_buf,
    loc_sem, a_send, a_recv, h_send, h_recv, g_send, g_recv,
    o_send, o_recv, o_loc, b1_send, b1_recv, b2_send, b2_recv,
):
    span = (2 * NB + 1) * frames
    ctxw = NB * frames
    own = GROUP * frames
    total_rows = own + 2 * ctxw
    score_scale = 1.0 / math.sqrt(HEAD)
    dp = lax.axis_index("dp")
    ctx = lax.axis_index("ctx")
    g = lax.div(ctx, GROUP)
    i = lax.rem(ctx, GROUP)
    n_peer = n_dp * n_groups
    slot = dp * n_groups + g
    has_lo = g > 0
    has_hi = g < n_groups - 1
    srcs = (q_hbm, k_hbm, v_hbm, g_hbm)
    outs = (att_out, gq_out, gk_out, gv_out)
    accs = (gk_acc, gv_acc)

    def group_dev(j):
        return {"dp": dp, "ctx": g * GROUP + j}

    def side_dev(direction):
        return {"dp": dp, "ctx": ctx + (GROUP if direction else -GROUP)}

    def peer_dev(s):
        return {"dp": lax.div(s, n_groups), "ctx": lax.rem(s, n_groups) * GROUP + i}

    def lanes(j, p):
        return pl.ds(pl.multiple_of((j * PAIRS + p) * LANES, LANES), LANES)

    def rows_of(arr, p, j):
        if arr in (K, V):
            start = pl.multiple_of(ctxw + j * frames, frames)
            return (kbuf if arr == K else vbuf).at[p, pl.ds(start, frames), :]
        start = pl.multiple_of(j * frames, frames)
        return (qbuf if arr == Q else gbuf).at[p, pl.ds(start, frames), :]

    def local_in(arr, p):
        return pltpu.make_async_copy(srcs[arr].at[0, :, lanes(i, p)], rows_of(arr, p, i), loc_sem.at[arr, p])

    def a_copy(arr, p, j):
        return pltpu.make_async_remote_copy(
            src_ref=srcs[arr].at[0, :, lanes(j, p)],
            dst_ref=rows_of(arr, p, i),
            send_sem=a_send.at[arr, p, j],
            recv_sem=a_recv.at[arr, p, i],
            device_id=group_dev(j),
            device_id_type=MESH,
        )

    def a_arrival(arr, p, j):
        return pltpu.make_async_remote_copy(
            src_ref=rows_of(arr, p, j),
            dst_ref=rows_of(arr, p, j),
            send_sem=a_send.at[arr, p, j],
            recv_sem=a_recv.at[arr, p, j],
            device_id=group_dev(j),
            device_id_type=MESH,
        )

    def halo_copy(a, p, direction):
        buf = (kbuf, vbuf)[a]
        src = own if direction else ctxw
        dst = 0 if direction else ctxw + own
        return pltpu.make_async_remote_copy(
            src_ref=buf.at[p, pl.ds(src, ctxw), :],
            dst_ref=buf.at[p, pl.ds(dst, ctxw), :],
            send_sem=h_send.at[a, p, direction],
            recv_sem=h_recv.at[a, p, direction],
            device_id=side_dev(direction),
            device_id_type=MESH,
        )

    def grad_copy(a, p, direction):
        return pltpu.make_async_remote_copy(
            src_ref=halo_out.at[a, p, direction],
            dst_ref=halo_in.at[a, p, direction],
            send_sem=g_send.at[a, p, direction],
            recv_sem=g_recv.at[a, p, direction],
            device_id=side_dev(direction),
            device_id_type=MESH,
        )

    def out_copy(arr, p, j):
        return pltpu.make_async_remote_copy(
            src_ref=ostage.at[arr, p, j],
            dst_ref=outs[arr].at[0, :, lanes(i, p)],
            send_sem=o_send.at[arr, p, j],
            recv_sem=o_recv.at[arr, p, i],
            device_id=group_dev(j),
            device_id_type=MESH,
        )

    def out_arrival(arr, p, j):
        return pltpu.make_async_remote_copy(
            src_ref=ostage.at[arr, p, j],
            dst_ref=outs[arr].at[0, :, lanes(j, p)],
            send_sem=o_send.at[arr, p, j],
            recv_sem=o_recv.at[arr, p, j],
            device_id=group_dev(j),
            device_id_type=MESH,
        )

    def out_local(arr, p):
        return pltpu.make_async_copy(ostage.at[arr, p, i], outs[arr].at[0, :, lanes(i, p)], o_loc.at[arr, p])

    def send_out(arr, p, j):
        @pl.when(j != i)
        def _():
            out_copy(arr, p, j).start()

        @pl.when(j == i)
        def _():
            out_local(arr, p).start()

    def b1_copy(p, s):
        return pltpu.make_async_remote_copy(
            src_ref=b1buf.at[slot, p],
            dst_ref=b1buf.at[slot, p],
            send_sem=b1_send.at[p, s],
            recv_sem=b1_recv.at[p, slot],
            device_id=peer_dev(s),
            device_id_type=MESH,
        )

    def b1_arrival(p, s):
        return pltpu.make_async_remote_copy(
            src_ref=b1buf.at[s, p],
            dst_ref=b1buf.at[s, p],
            send_sem=b1_send.at[p, s],
            recv_sem=b1_recv.at[p, s],
            device_id=peer_dev(s),
            device_id_type=MESH,
        )

    def b2_copy(p, j):
        return pltpu.make_async_remote_copy(
            src_ref=sum_buf.at[p],
            dst_ref=b2buf.at[i, p],
            send_sem=b2_send.at[p, j],
            recv_sem=b2_recv.at[p, i],
            device_id=group_dev(j),
            device_id_type=MESH,
        )

    def b2_arrival(p, j):
        return pltpu.make_async_remote_copy(
            src_ref=sum_buf.at[p],
            dst_ref=b2buf.at[j, p],
            send_sem=b2_send.at[p, j],
            recv_sem=b2_recv.at[p, j],
            device_id=group_dev(j),
            device_id_type=MESH,
        )

    def others(fn):
        for s in range(1, GROUP):
            fn(lax.rem(i + s, GROUP))

    def all_peers(fn):
        def step(t, carry):
            fn(lax.rem(slot + t, n_peer))
            return carry

        lax.fori_loop(1, n_peer, step, 0)

    barrier = pltpu.get_barrier_semaphore()

    def greet(device):
        pl.semaphore_signal(barrier, inc=1, device_id=device, device_id_type=MESH)

    others(lambda j: greet(group_dev(j)))
    all_peers(lambda s: greet(peer_dev(s)))
    for p in range(PAIRS):
        for arr in (K, V, Q, G):
            local_in(arr, p).start()
    pl.semaphore_wait(barrier, GROUP - 1 + n_peer - 1)

    for p in range(PAIRS):
        for arr in (K, V, Q, G):
            others(lambda j: a_copy(arr, p, j).start())

    for p in range(PAIRS):
        for h in range(2):
            row = rev_ref[pl.ds(i * (2 * PAIRS) + 2 * p + h, 1), :]
            table = jnp.broadcast_to(row, (frames, span))
            bias_tab[p, h * frames : (h + 1) * frames, :] = pltpu.roll(
                table, 0, 1, stride=1, stride_axis=0
            )
    bias_acc[...] = jnp.zeros_like(bias_acc)
    gk_acc[...] = jnp.zeros_like(gk_acc)
    gv_acc[...] = jnp.zeros_like(gv_acc)
    edge_zero = jnp.zeros((PAIRS, ctxw, LANES), jnp.bfloat16)

    @pl.when(jnp.logical_not(has_lo))
    def _():
        kbuf[:, :ctxw, :] = edge_zero
        vbuf[:, :ctxw, :] = edge_zero

    @pl.when(jnp.logical_not(has_hi))
    def _():
        kbuf[:, ctxw + own :, :] = edge_zero
        vbuf[:, ctxw + own :, :] = edge_zero

    def forward_halo(p):
        for a, arr in enumerate((K, V)):
            local_in(arr, p).wait()
            others(lambda j: a_arrival(arr, p, j).wait_recv())

            @pl.when(has_lo)
            def _():
                halo_copy(a, p, 0).start()

            @pl.when(has_hi)
            def _():
                halo_copy(a, p, 1).start()

    def wait_inputs(p):
        for arr in (Q, G):
            local_in(arr, p).wait()
            others(lambda j: a_arrival(arr, p, j).wait_recv())
        for a in range(2):
            @pl.when(has_lo)
            def _():
                halo_copy(a, p, 1).wait_recv()

            @pl.when(has_hi)
            def _():
                halo_copy(a, p, 0).wait_recv()

    low = lax.broadcasted_iota(jnp.int32, (frames, LANES), 1) < HEAD

    def stack_heads(x):
        zero = jnp.zeros_like(x)
        return jnp.concatenate([jnp.where(low, x, zero), jnp.where(low, zero, x)], axis=0)

    def merge_heads(x):
        return jnp.where(low, x[:frames], x[frames:])

    column = lax.broadcasted_iota(jnp.int32, (1, span), 1)

    def unit(p, b):
        r0 = pl.multiple_of(b * frames, frames)
        own_rows = pl.ds(r0, frames)
        window = pl.ds(r0, span)
        key_row = column + ((g * GROUP - NB + b) * frames)
        exists = (key_row >= 0) & (key_row < n_groups * own)
        edge = jnp.where(exists, 0.0, EXCLUDED).astype(jnp.float32)
        kw = kbuf[p, window, :]
        vw = vbuf[p, window, :]
        qs = stack_heads(qbuf[p, own_rows, :].astype(jnp.float32) * score_scale).astype(jnp.bfloat16)
        gs = stack_heads(gbuf[p, own_rows, :].astype(jnp.float32)).astype(jnp.bfloat16)
        scores = dot(qs, kw, NT) + bias_tab[p] + edge
        top = jnp.max(scores, axis=1, keepdims=True)
        expd = jnp.exp(scores - top)
        total = jnp.sum(expd, axis=1, keepdims=True)
        probs = expd * (1.0 / total)
        weights = probs.astype(jnp.bfloat16)
        attended = merge_heads(dot(weights, vw)).astype(jnp.bfloat16)
        ostage[0, p, b] = attended
        send_out(0, p, b)
        wide = attended.astype(jnp.float32)
        delta = jnp.sum(
            gs.astype(jnp.float32) * jnp.concatenate([wide, wide], axis=0), axis=1, keepdims=True
        )
        dscore = probs * (dot(gs, vw, NT) - delta)
        dscore_low = dscore.astype(jnp.bfloat16)
        bias_acc[p] += dscore
        grad_q = merge_heads(dot(dscore_low, kw)) * score_scale
        ostage[1, p, b] = grad_q.astype(jnp.bfloat16)
        send_out(1, p, b)
        gk_acc[p, window, :] += dot(dscore_low, qs, TN)
        gv_acc[p, window, :] += dot(weights, gs, TN)

    def send_grads(p):
        for a in range(2):
            @pl.when(has_lo)
            def _():
                halo_out[a, p, 0] = accs[a][p, :ctxw, :].astype(jnp.bfloat16)
                grad_copy(a, p, 0).start()

            @pl.when(has_hi)
            def _():
                halo_out[a, p, 1] = accs[a][p, ctxw + own :, :].astype(jnp.bfloat16)
                grad_copy(a, p, 1).start()

    def send_bias(p):
        sub = lax.broadcasted_iota(jnp.int32, (8, span), 0)
        b1buf[slot, p] = jnp.zeros((16, 128), jnp.float32)
        for h in range(2):
            part = bias_acc[p, h * frames : (h + 1) * frames, :]
            rows = frames
            while rows > 8:
                rows //= 2
                part = part[:rows] + pltpu.roll(part[rows:], span - rows, 1)
            for s in (4, 2, 1):
                part = jnp.where((sub & s) != 0, pltpu.roll(part, span - s, 1), part)
            diag = jnp.sum(part, axis=0, keepdims=True)
            for c in range(span // 128):
                n = h * (span // 128) + c
                b1buf[slot, p, n : n + 1, :] = diag[:, c * 128 : (c + 1) * 128]
        all_peers(lambda s: b1_copy(p, s).start())

    def sum_bias(p):
        all_peers(lambda s: b1_arrival(p, s).wait_recv())
        sum_buf[p] = lax.fori_loop(
            0, n_peer, lambda s, acc: acc + b1buf[s, p], jnp.zeros((16, 128), jnp.float32)
        )
        others(lambda j: b2_copy(p, j).start())
        b2buf[i, p] = sum_buf[p]

    def finish_grads(p):
        for a in range(2):
            acc = accs[a]

            @pl.when(has_lo)
            def _():
                grad_copy(a, p, 1).wait_recv()
                acc[p, ctxw : 2 * ctxw, :] += halo_in[a, p, 1].astype(jnp.float32)

            @pl.when(has_hi)
            def _():
                grad_copy(a, p, 0).wait_recv()
                acc[p, own : own + ctxw, :] += halo_in[a, p, 0].astype(jnp.float32)

            for j in range(GROUP):
                start = ctxw + j * frames
                ostage[2 + a, p, j] = acc[p, start : start + frames, :].astype(jnp.bfloat16)
                send_out(2 + a, p, j)

    forward_halo(0)
    for p in range(PAIRS):
        wait_inputs(p)

        def step(b, carry):
            unit(p, b)

            @pl.when(b == 1)
            def _():
                if p + 1 < PAIRS:
                    forward_halo(p + 1)
                if p > 0:
                    sum_bias(p - 1)
                    finish_grads(p - 1)

            return carry

        lax.fori_loop(0, GROUP, step, 0)
        send_grads(p)
        send_bias(p)
    finish_grads(PAIRS - 1)
    sum_bias(PAIRS - 1)

    for p in range(PAIRS):
        others(lambda j: b2_arrival(p, j).wait_recv())
    bias_out[...] = b2buf[...]
    for p in range(PAIRS):
        for arr in range(4):
            others(lambda j: out_arrival(arr, p, j).wait_recv())
            out_local(arr, p).wait()
            others(lambda j: out_copy(arr, p, j).wait_send())
            others(lambda j: a_copy(arr, p, j).wait_send())
        for a in range(2):
            @pl.when(has_lo)
            def _():
                halo_copy(a, p, 0).wait_send()
                grad_copy(a, p, 0).wait_send()

            @pl.when(has_hi)
            def _():
                halo_copy(a, p, 1).wait_send()
                grad_copy(a, p, 1).wait_send()

        all_peers(lambda s: b1_copy(p, s).wait_send())
        others(lambda j: b2_copy(p, j).wait_send())


def body(queries, keys, values, rel_bias, grad_out):
    rec_dev, frames, width = queries.shape
    n_dp = lax.axis_size("dp")
    n_groups = lax.axis_size("ctx") // GROUP
    n_peer = n_dp * n_groups
    span = (2 * NB + 1) * frames
    ctxw = NB * frames
    own = GROUP * frames
    rows = own + 2 * ctxw
    count = 2 * ctxw + 1
    reversed_bias = jnp.pad(
        rel_bias[:, ::-1], ((0, 0), (0, span - count)), constant_values=EXCLUDED
    )
    block = jax.ShapeDtypeStruct(queries.shape, jnp.bfloat16)
    bf16, f32 = jnp.bfloat16, jnp.float32
    dma = pltpu.SemaphoreType.DMA
    hbm = pl.BlockSpec(memory_space=pl.ANY)
    vmem = pl.BlockSpec(memory_space=pltpu.VMEM)
    macs = 6 * GROUP * frames * span * 2 * PAIRS * HEAD
    att, gq, gk, gv, bias = pl.pallas_call(
        functools.partial(kernel, n_dp, n_groups, frames),
        out_shape=(block, block, block, block, jax.ShapeDtypeStruct((GROUP, PAIRS, 16, 128), f32)),
        in_specs=[hbm, hbm, hbm, hbm, vmem],
        out_specs=(hbm, hbm, hbm, hbm, vmem),
        scratch_shapes=[
            pltpu.VMEM((PAIRS, own, LANES), bf16),
            pltpu.VMEM((PAIRS, own, LANES), bf16),
            pltpu.VMEM((PAIRS, rows, LANES), bf16),
            pltpu.VMEM((PAIRS, rows, LANES), bf16),
            pltpu.VMEM((PAIRS, 2 * frames, span), f32),
            pltpu.VMEM((PAIRS, 2 * frames, span), f32),
            pltpu.VMEM((PAIRS, rows, LANES), f32),
            pltpu.VMEM((PAIRS, rows, LANES), f32),
            pltpu.VMEM((2, PAIRS, 2, ctxw, LANES), bf16),
            pltpu.VMEM((2, PAIRS, 2, ctxw, LANES), bf16),
            pltpu.VMEM((4, PAIRS, GROUP, frames, LANES), bf16),
            pltpu.VMEM((n_peer, PAIRS, 16, 128), f32),
            pltpu.VMEM((GROUP, PAIRS, 16, 128), f32),
            pltpu.VMEM((PAIRS, 16, 128), f32),
            dma((4, PAIRS)),
            dma((4, PAIRS, GROUP)),
            dma((4, PAIRS, GROUP)),
            dma((2, PAIRS, 2)),
            dma((2, PAIRS, 2)),
            dma((2, PAIRS, 2)),
            dma((2, PAIRS, 2)),
            dma((4, PAIRS, GROUP)),
            dma((4, PAIRS, GROUP)),
            dma((4, PAIRS)),
            dma((PAIRS, n_peer)),
            dma((PAIRS, n_peer)),
            dma((PAIRS, GROUP)),
            dma((PAIRS, GROUP)),
        ],
        compiler_params=pltpu.CompilerParams(
            collective_id=0, has_side_effects=True, vmem_limit_bytes=48 * 1024 * 1024
        ),
        cost_estimate=pl.CostEstimate(
            flops=2 * macs, bytes_accessed=8 * frames * width * 2, transcendentals=own * span * 2 * PAIRS
        ),
    )(queries, keys, values, grad_out, reversed_bias)
    tiles = 2 * (span // 128)
    table = bias[:, :, :tiles, :].reshape(HEADS, span)
    grad_bias = table[:, :count][:, ::-1]
    return (att, gq, gk, gv, grad_bias)


def solution(mesh):
    placed = (
        P("dp", "ctx", None),
        P("dp", "ctx", None),
        P("dp", "ctx", None),
        P(),
        P("dp", "ctx", None),
    )
    return jax.shard_map(
        body,
        mesh=mesh,
        in_specs=placed,
        out_specs=(
            P("dp", "ctx", None),
            P("dp", "ctx", None),
            P("dp", "ctx", None),
            P("dp", "ctx", None),
            P(),
        ),
        check_vma=False,
    )
```

profile of v0, /device:TPU:0, one launch (start us, length us, event | category | flops | bytes accessed | tf_op | source)
XLA Modules:
  0.0 58.3 jit_solution(18081251126239684919)
XLA Ops:
  0.6 0.0 copy-start
  0.6 3.1 %reverse = f32[16,896]{1,0:T(8,128)S(1)} reverse(f32[16,896]{1,0:T(8,128)} %bitcast.5), dimensions={1} | reverse | bytes 114688
  3.8 0.1 slice.9
  3.8 0.0 copy-done
  3.9 0.0 copy-start.1
  3.9 0.9 %copy-done.1 = bf16[1,128,1024]{2,1,0:T(8,128)(2,1)S(1)} copy-done((bf16[1,128,1024]{2,1,0:T(8,128)(2,1)S(1)}, bf16[1,128,1024]{2,1,0:T(8,128)(2,1)}, u32[]{:S(2)}) %copy-start.1) | copy-done | bytes 262168
  4.8 0.0 copy-start.2
  4.8 0.9 %copy-done.2 = bf16[1,128,1024]{2,1,0:T(8,128)(2,1)S(1)} copy-done((bf16[1,128,1024]{2,1,0:T(8,128)(2,1)S(1)}, bf16[1,128,1024]{2,1,0:T(8,128)(2,1)}, u32[]{:S(2)}) %copy-start.2) | copy-done | bytes 262168
  5.8 0.0 copy-start.3
  5.8 0.9 %copy-done.3 = bf16[1,128,1024]{2,1,0:T(8,128)(2,1)S(1)} copy-done((bf16[1,128,1024]{2,1,0:T(8,128)(2,1)S(1)}, bf16[1,128,1024]{2,1,0:T(8,128)(2,1)}, u32[]{:S(2)}) %copy-start.3) | copy-done | bytes 262168
  6.7 47.5 %shard_map.92 = (bf16[1,128,1024]{2,1,0:T(8,128)(2,1)S(1)}, bf16[1,128,1024]{2,1,0:T(8,128)(2,1)S(1)}, bf16[1,128,1024]{2,1,0:T(8,128)(2,1)S(1)}, bf16[1,128,1024]{2,1,0:T(8,128)(2,1)S(1)}, f32[4,2,16,128]{3,2,1,0:T(8,128)S(1)}) custom-call(bf16[1,128,1024]{2,1,0:T(8,128)(2,1)S(1)} %copy-done, bf16[1,128,1024]{2,1,0:T(8,128)(2,1)S(1)} %copy-done.1, ...), custom_call_target="tpu_custom_call" | custom-call | flops 1409286144 | bytes 2097152 | tf_op jit(solution)/shard_map/pallas_call | solution.py:432
  54.2 0.5 reverse.1
  54.8 0.7 %slice.10 = f32[16,769]{1,0:T(8,128)} slice(f32[16,896]{1,0:T(8,128)S(1)} %reverse.1), slice={[0:16], [127:896]} | slice | bytes 98432
  55.5 0.7 %copy.14 = bf16[1,128,1024]{2,1,0:T(8,128)(2,1)} copy(bf16[1,128,1024]{2,1,0:T(8,128)(2,1)S(1)} %get-tuple-element.20) | data formatting | bytes 524288
  56.2 0.7 %copy.15 = bf16[1,128,1024]{2,1,0:T(8,128)(2,1)} copy(bf16[1,128,1024]{2,1,0:T(8,128)(2,1)S(1)} %get-tuple-element.21) | data formatting | bytes 524288
  56.9 0.7 %copy.16 = bf16[1,128,1024]{2,1,0:T(8,128)(2,1)} copy(bf16[1,128,1024]{2,1,0:T(8,128)(2,1)S(1)} %get-tuple-element.22) | data formatting | bytes 524288
  57.6 0.7 %copy.17 = bf16[1,128,1024]{2,1,0:T(8,128)(2,1)} copy(bf16[1,128,1024]{2,1,0:T(8,128)(2,1)S(1)} %get-tuple-element.23) | data formatting | bytes 524288
  (2 shorter events, 0.0 us)
Async XLA Ops:
  0.6 3.2 %copy-start = (bf16[1,128,1024]{2,1,0:T(8,128)(2,1)S(1)}, bf16[1,128,1024]{2,1,0:T(8,128)(2,1)}, u32[]{:S(2)}) copy-start(bf16[1,128,1024]{2,1,0:T(8,128)(2,1)} %q_hbm.1) | copy-start | bytes 786436
  3.9 1.0 %copy-start.1 = (bf16[1,128,1024]{2,1,0:T(8,128)(2,1)S(1)}, bf16[1,128,1024]{2,1,0:T(8,128)(2,1)}, u32[]{:S(2)}) copy-start(bf16[1,128,1024]{2,1,0:T(8,128)(2,1)} %k_hbm.1) | copy-start | bytes 786436
  4.8 0.9 %copy-start.2 = (bf16[1,128,1024]{2,1,0:T(8,128)(2,1)S(1)}, bf16[1,128,1024]{2,1,0:T(8,128)(2,1)}, u32[]{:S(2)}) copy-start(bf16[1,128,1024]{2,1,0:T(8,128)(2,1)} %v_hbm.1) | copy-start | bytes 786436
  5.8 0.9 %copy-start.3 = (bf16[1,128,1024]{2,1,0:T(8,128)(2,1)S(1)}, bf16[1,128,1024]{2,1,0:T(8,128)(2,1)}, u32[]{:S(2)}) copy-start(bf16[1,128,1024]{2,1,0:T(8,128)(2,1)} %g_hbm.1) | copy-start | bytes 786436
where the time goes:
time: 58.6 us; the launch traced here: 58.3 us
  Pallas kernels  47.5 us (81%)
  local copies, waits for them, and re-layouts  10.1 us (17%)
  between operations  0.68 us (1%)
    pallas_call x1, Pallas kernels, body(): pl.pallas_call(functools.partial(kernel, n_dp, n_groups, frames), out_sha...  47.5 us
    unnamed x16, local copies, waits for them, and re-layouts  10.1 us

commit v1 on v0

--- a/solution.py
+++ b/solution.py
@@ -15,29 +15,41 @@
 PAIRS = HEADS // GROUP // 2
 LANES = 2 * HEAD
 EXCLUDED = -1e30
+VMEM_LIMIT = 60 * 1024 * 1024
 MESH = pl.DeviceIdType.MESH
 Q, K, V, G = 0, 1, 2, 3
 NT = (((1,), (1,)), ((), ()))
-TN = (((0,), (0,)), ((), ()))
+
+
+ORDER = (0, 3, 1, 2)
+DONE = {0: ((0, 0),), 3: ((1, 2),), 1: ((0, 1),), 2: ((1, 0), (1, 1), (0, 2))}
 
 
 def dot(a, b, dims=(((1,), (0,)), ((), ()))):
     return lax.dot_general(a, b, dims, preferred_element_type=jnp.float32)
 
 
+def mirror_lanes(x):
+    row = lax.broadcasted_iota(jnp.int32, (128, 128), 0)
+    col = lax.broadcasted_iota(jnp.int32, (128, 128), 1)
+    exchange = (row + col == 127).astype(jnp.float32)
+    return jnp.dot(
+        x, exchange, precision=lax.Precision.HIGHEST, preferred_element_type=jnp.float32
+    )
+
+
 def kernel(
     n_dp, n_groups, frames,
-    q_hbm, k_hbm, v_hbm, g_hbm, rev_ref,
+    q_hbm, k_hbm, v_hbm, g_hbm, rel_ref,
     att_out, gq_out, gk_out, gv_out, bias_out,
-    qbuf, gbuf, kbuf, vbuf, bias_tab, bias_acc, gk_acc, gv_acc,
-    halo_out, halo_in, ostage, b1buf, b2buf, sum_buf,
+    qbuf, gbuf, kbuf, vbuf, rev_buf, bias_tab, bias_acc, gk_acc, gv_acc,
+    ds_buf, w_buf, qt_buf, gt_buf, halo_out, halo_in, ostage, b1buf, sum_buf,
     loc_sem, a_send, a_recv, h_send, h_recv, g_send, g_recv,
     o_send, o_recv, o_loc, b1_send, b1_recv, b2_send, b2_recv,
 ):
     span = (2 * NB + 1) * frames
     ctxw = NB * frames
     own = GROUP * frames
-    total_rows = own + 2 * ctxw
     score_scale = 1.0 / math.sqrt(HEAD)
     dp = lax.axis_index("dp")
     ctx = lax.axis_index("ctx")
@@ -93,25 +105,26 @@
             device_id_type=MESH,
         )
 
-    def halo_copy(a, p, direction):
+    def halo_copy(a, p, direction, j):
         buf = (kbuf, vbuf)[a]
-        src = own if direction else ctxw
-        dst = 0 if direction else ctxw + own
-        return pltpu.make_async_remote_copy(
-            src_ref=buf.at[p, pl.ds(src, ctxw), :],
-            dst_ref=buf.at[p, pl.ds(dst, ctxw), :],
-            send_sem=h_send.at[a, p, direction],
-            recv_sem=h_recv.at[a, p, direction],
+        src = pl.multiple_of(ctxw + j * frames, frames)
+        place = j - 1 if direction else j
+        dst = pl.multiple_of(place * frames + (0 if direction else ctxw + own), frames)
+        return pltpu.make_async_remote_copy(
+            src_ref=buf.at[p, pl.ds(src, frames), :],
+            dst_ref=buf.at[p, pl.ds(dst, frames), :],
+            send_sem=h_send.at[a, p, direction, place],
+            recv_sem=h_recv.at[a, p, direction, place],
             device_id=side_dev(direction),
             device_id_type=MESH,
         )
 
-    def grad_copy(a, p, direction):
-        return pltpu.make_async_remote_copy(
-            src_ref=halo_out.at[a, p, direction],
-            dst_ref=halo_in.at[a, p, direction],
-            send_sem=g_send.at[a, p, direction],
-            recv_sem=g_recv.at[a, p, direction],
+    def grad_copy(a, p, direction, blk):
+        return pltpu.make_async_remote_copy(
+            src_ref=halo_out.at[a, p, direction, blk],
+            dst_ref=halo_in.at[a, p, direction, blk],
+            send_sem=g_send.at[a, p, direction, blk],
+            recv_sem=g_recv.at[a, p, direction, blk],
             device_id=side_dev(direction),
             device_id_type=MESH,
         )
@@ -171,7 +184,7 @@
     def b2_copy(p, j):
         return pltpu.make_async_remote_copy(
             src_ref=sum_buf.at[p],
-            dst_ref=b2buf.at[i, p],
+            dst_ref=bias_out.at[i, p],
             send_sem=b2_send.at[p, j],
             recv_sem=b2_recv.at[p, i],
             device_id=group_dev(j),
@@ -181,7 +194,7 @@
     def b2_arrival(p, j):
         return pltpu.make_async_remote_copy(
             src_ref=sum_buf.at[p],
-            dst_ref=b2buf.at[j, p],
+            dst_ref=bias_out.at[j, p],
             send_sem=b2_send.at[p, j],
             recv_sem=b2_recv.at[p, j],
             device_id=group_dev(j),
@@ -189,8 +202,11 @@
         )
 
     def others(fn):
-        for s in range(1, GROUP):
-            fn(lax.rem(i + s, GROUP))
+        core = lax.rem(i, 2)
+        far = 2 - 2 * lax.div(i, 2)
+        fn(i + 1 - 2 * core)
+        fn(far + core)
+        fn(far + 1 - core)
 
     def all_peers(fn):
         def step(t, carry):
@@ -215,40 +231,60 @@
         for arr in (K, V, Q, G):
             others(lambda j: a_copy(arr, p, j).start())
 
+    chunks = 2 * ctxw // 128
+    for c in range(chunks):
+        rev_buf[:, (chunks - 1 - c) * 128 : (chunks - c) * 128] = mirror_lanes(
+            rel_ref[:, c * 128 : (c + 1) * 128]
+        )
+    last_lane = lax.broadcasted_iota(jnp.int32, (HEADS, 128), 1) == 127
+    rev_buf[:, 2 * ctxw :] = jnp.where(
+        last_lane, rel_ref[:, 2 * ctxw : 2 * ctxw + 1], jnp.float32(EXCLUDED)
+    )
     for p in range(PAIRS):
         for h in range(2):
-            row = rev_ref[pl.ds(i * (2 * PAIRS) + 2 * p + h, 1), :]
+            row = rev_buf[pl.ds(i * (2 * PAIRS) + 2 * p + h, 1), :]
             table = jnp.broadcast_to(row, (frames, span))
             bias_tab[p, h * frames : (h + 1) * frames, :] = pltpu.roll(
-                table, 0, 1, stride=1, stride_axis=0
+                table, 1, 1, stride=1, stride_axis=0
             )
     bias_acc[...] = jnp.zeros_like(bias_acc)
     gk_acc[...] = jnp.zeros_like(gk_acc)
     gv_acc[...] = jnp.zeros_like(gv_acc)
     edge_zero = jnp.zeros((PAIRS, ctxw, LANES), jnp.bfloat16)
+    edge_grad = jnp.zeros((2, PAIRS, NB, LANES, frames), jnp.bfloat16)
 
     @pl.when(jnp.logical_not(has_lo))
     def _():
         kbuf[:, :ctxw, :] = edge_zero
         vbuf[:, :ctxw, :] = edge_zero
+        halo_in[:, :, 1] = edge_grad
 
     @pl.when(jnp.logical_not(has_hi))
     def _():
         kbuf[:, ctxw + own :, :] = edge_zero
         vbuf[:, ctxw + own :, :] = edge_zero
+        halo_in[:, :, 0] = edge_grad
 
     def forward_halo(p):
+        def forward(a, j):
+            @pl.when(has_lo & (j < NB))
+            def _():
+                halo_copy(a, p, 0, j).start()
+
+            @pl.when(has_hi & (j > 0))
+            def _():
+                halo_copy(a, p, 1, j).start()
+
         for a, arr in enumerate((K, V)):
             local_in(arr, p).wait()
-            others(lambda j: a_arrival(arr, p, j).wait_recv())
-
-            @pl.when(has_lo)
-            def _():
-                halo_copy(a, p, 0).start()
-
-            @pl.when(has_hi)
-            def _():
-                halo_copy(a, p, 1).start()
+            forward(a, i)
+
+        def passed_on(j):
+            for a, arr in enumerate((K, V)):
+                a_arrival(arr, p, j).wait_recv()
+                forward(a, j)
+
+        others(passed_on)
 
     def wait_inputs(p):
         for arr in (Q, G):
@@ -257,11 +293,13 @@
         for a in range(2):
             @pl.when(has_lo)
             def _():
-                halo_copy(a, p, 1).wait_recv()
+                for j in range(1, GROUP):
+                    halo_copy(a, p, 1, j).wait_recv()
 
             @pl.when(has_hi)
             def _():
-                halo_copy(a, p, 0).wait_recv()
+                for j in range(NB):
+                    halo_copy(a, p, 0, j).wait_recv()
 
     low = lax.broadcasted_iota(jnp.int32, (frames, LANES), 1) < HEAD
 
@@ -274,50 +312,65 @@
 
     column = lax.broadcasted_iota(jnp.int32, (1, span), 1)
 
-    def unit(p, b):
-        r0 = pl.multiple_of(b * frames, frames)
-        own_rows = pl.ds(r0, frames)
-        window = pl.ds(r0, span)
+    top_half = lax.broadcasted_iota(jnp.int32, (LANES, frames), 0) < HEAD
+
+    def stack_turned(x):
+        turned = x.T
+        zero = jnp.zeros_like(turned)
+        return jnp.concatenate(
+            [jnp.where(top_half, turned, zero), jnp.where(top_half, zero, turned)], axis=1
+        ).astype(jnp.bfloat16)
+
+    def softmax_part(n, p, b):
+        own_rows = slice(b * frames, (b + 1) * frames)
+        window = slice(b * frames, b * frames + span)
         key_row = column + ((g * GROUP - NB + b) * frames)
         exists = (key_row >= 0) & (key_row < n_groups * own)
         edge = jnp.where(exists, 0.0, EXCLUDED).astype(jnp.float32)
         kw = kbuf[p, window, :]
         vw = vbuf[p, window, :]
-        qs = stack_heads(qbuf[p, own_rows, :].astype(jnp.float32) * score_scale).astype(jnp.bfloat16)
-        gs = stack_heads(gbuf[p, own_rows, :].astype(jnp.float32)).astype(jnp.bfloat16)
+        q32 = qbuf[p, own_rows, :].astype(jnp.float32) * score_scale
+        g32 = gbuf[p, own_rows, :].astype(jnp.float32)
+        qs = stack_heads(q32).astype(jnp.bfloat16)
+        gs32 = stack_heads(g32)
+        gs = gs32.astype(jnp.bfloat16)
+        qt_buf[n % 2] = stack_turned(q32)
+        gt_buf[n % 2] = stack_turned(g32)
         scores = dot(qs, kw, NT) + bias_tab[p] + edge
         top = jnp.max(scores, axis=1, keepdims=True)
         expd = jnp.exp(scores - top)
         total = jnp.sum(expd, axis=1, keepdims=True)
         probs = expd * (1.0 / total)
         weights = probs.astype(jnp.bfloat16)
+        w_buf[n % 2] = weights
         attended = merge_heads(dot(weights, vw)).astype(jnp.bfloat16)
         ostage[0, p, b] = attended
-        send_out(0, p, b)
         wide = attended.astype(jnp.float32)
-        delta = jnp.sum(
-            gs.astype(jnp.float32) * jnp.concatenate([wide, wide], axis=0), axis=1, keepdims=True
-        )
+        delta = jnp.sum(gs32 * jnp.concatenate([wide, wide], axis=0), axis=1, keepdims=True)
         dscore = probs * (dot(gs, vw, NT) - delta)
-        dscore_low = dscore.astype(jnp.bfloat16)
+        ds_buf[n % 2] = dscore.astype(jnp.bfloat16)
         bias_acc[p] += dscore
-        grad_q = merge_heads(dot(dscore_low, kw)) * score_scale
+
+    def grad_part(n, p, b):
+        window = slice(b * frames, b * frames + span)
+        dscore_low = ds_buf[n % 2]
+        grad_q = merge_heads(dot(dscore_low, kbuf[p, window, :])) * score_scale
         ostage[1, p, b] = grad_q.astype(jnp.bfloat16)
+        gk_acc[p, :, window] += dot(qt_buf[n % 2], dscore_low)
+        gv_acc[p, :, window] += dot(gt_buf[n % 2], w_buf[n % 2])
+
+    def send_grads(p, b):
         send_out(1, p, b)
-        gk_acc[p, window, :] += dot(dscore_low, qs, TN)
-        gv_acc[p, window, :] += dot(weights, gs, TN)
-
-    def send_grads(p):
-        for a in range(2):
-            @pl.when(has_lo)
-            def _():
-                halo_out[a, p, 0] = accs[a][p, :ctxw, :].astype(jnp.bfloat16)
-                grad_copy(a, p, 0).start()
-
-            @pl.when(has_hi)
-            def _():
-                halo_out[a, p, 1] = accs[a][p, ctxw + own :, :].astype(jnp.bfloat16)
-                grad_copy(a, p, 1).start()
+        for direction, blk in DONE[b]:
+            start = blk * frames + (ctxw + own if direction else 0)
+
+            @pl.when(has_hi if direction else has_lo)
+            def _():
+                for a in range(2):
+                    halo_out[a, p, direction, blk] = accs[a][p, :, start : start + frames].astype(
+                        jnp.bfloat16
+                    )
+                    grad_copy(a, p, direction, blk).start()
 
     def send_bias(p):
         sub = lax.broadcasted_iota(jnp.int32, (8, span), 0)
@@ -330,7 +383,7 @@
                 part = part[:rows] + pltpu.roll(part[rows:], span - rows, 1)
             for s in (4, 2, 1):
                 part = jnp.where((sub & s) != 0, pltpu.roll(part, span - s, 1), part)
-            diag = jnp.sum(part, axis=0, keepdims=True)
+            diag = pltpu.roll(jnp.sum(part, axis=0, keepdims=True), span - 1, 1)
             for c in range(span // 128):
                 n = h * (span // 128) + c
                 b1buf[slot, p, n : n + 1, :] = diag[:, c * 128 : (c + 1) * 128]
@@ -342,53 +395,55 @@
             0, n_peer, lambda s, acc: acc + b1buf[s, p], jnp.zeros((16, 128), jnp.float32)
         )
         others(lambda j: b2_copy(p, j).start())
-        b2buf[i, p] = sum_buf[p]
+        bias_out[i, p] = sum_buf[p]
 
     def finish_grads(p):
-        for a in range(2):
-            acc = accs[a]
-
-            @pl.when(has_lo)
-            def _():
-                grad_copy(a, p, 1).wait_recv()
-                acc[p, ctxw : 2 * ctxw, :] += halo_in[a, p, 1].astype(jnp.float32)
-
-            @pl.when(has_hi)
-            def _():
-                grad_copy(a, p, 0).wait_recv()
-                acc[p, own : own + ctxw, :] += halo_in[a, p, 0].astype(jnp.float32)
-
-            for j in range(GROUP):
+        for j in (2, 0, 1, 3):
+            for a in range(2):
+                if j < NB:
+                    @pl.when(has_lo)
+                    def _():
+                        grad_copy(a, p, 1, j).wait_recv()
+                if j > 0:
+                    @pl.when(has_hi)
+                    def _():
+                        grad_copy(a, p, 0, j - 1).wait_recv()
                 start = ctxw + j * frames
-                ostage[2 + a, p, j] = acc[p, start : start + frames, :].astype(jnp.bfloat16)
+                full = accs[a][p, :, start : start + frames]
+                if j < NB:
+                    full = full + halo_in[a, p, 1, j].astype(jnp.float32)
+                if j > 0:
+                    full = full + halo_in[a, p, 0, j - 1].astype(jnp.float32)
+                ostage[2 + a, p, j] = full.T.astype(jnp.bfloat16)
                 send_out(2 + a, p, j)
 
+    units = [(p, b) for p in range(PAIRS) for b in ORDER]
     forward_halo(0)
-    for p in range(PAIRS):
-        wait_inputs(p)
-
-        def step(b, carry):
-            unit(p, b)
-
-            @pl.when(b == 1)
-            def _():
-                if p + 1 < PAIRS:
-                    forward_halo(p + 1)
-                if p > 0:
-                    sum_bias(p - 1)
-                    finish_grads(p - 1)
-
-            return carry
-
-        lax.fori_loop(0, GROUP, step, 0)
-        send_grads(p)
-        send_bias(p)
+    for n, (p, b) in enumerate(units):
+        if b == ORDER[0]:
+            wait_inputs(p)
+        softmax_part(n, p, b)
+        if n > 0:
+            grad_part(n - 1, *units[n - 1])
+        send_out(0, p, b)
+        if n > 0:
+            send_grads(*units[n - 1])
+        if b == ORDER[0]:
+            if p + 1 < PAIRS:
+                forward_halo(p + 1)
+            if p > 0:
+                send_bias(p - 1)
+        if b == ORDER[2] and p > 0:
+            sum_bias(p - 1)
+            finish_grads(p - 1)
+    send_bias(PAIRS - 1)
+    grad_part(len(units) - 1, *units[-1])
+    send_grads(*units[-1])
+    sum_bias(PAIRS - 1)
     finish_grads(PAIRS - 1)
-    sum_bias(PAIRS - 1)
 
     for p in range(PAIRS):
         others(lambda j: b2_arrival(p, j).wait_recv())
-    bias_out[...] = b2buf[...]
     for p in range(PAIRS):
         for arr in range(4):
             others(lambda j: out_arrival(arr, p, j).wait_recv())
@@ -398,16 +453,39 @@
         for a in range(2):
             @pl.when(has_lo)
             def _():
-                halo_copy(a, p, 0).wait_send()
-                grad_copy(a, p, 0).wait_send()
+                for j in range(NB):
+                    halo_copy(a, p, 0, j).wait_send()
+                    grad_copy(a, p, 0, j).wait_send()
 
             @pl.when(has_hi)
             def _():
-                halo_copy(a, p, 1).wait_send()
-                grad_copy(a, p, 1).wait_send()
+                for j in range(NB):
+                    halo_copy(a, p, 1, j + 1).wait_send()
+                    grad_copy(a, p, 1, j).wait_send()
 
         all_peers(lambda s: b1_copy(p, s).wait_send())
         others(lambda j: b2_copy(p, j).wait_send())
+
+
+def finish(att, gq, gk, gv, bias, att_out, gq_out, gk_out, gv_out, bias_out, sems):
+    copies = [
+        pltpu.make_async_copy(src, dst, sems.at[n])
+        for n, (src, dst) in enumerate(
+            ((att, att_out), (gq, gq_out), (gk, gk_out), (gv, gv_out))
+        )
+    ]
+    for copy in copies:
+        copy.start()
+    chunks = bias_out.shape[1] // 128
+    mirrored = mirror_lanes(bias[...].reshape(GROUP * PAIRS * 16, 128))
+    for head in range(HEADS):
+        base = (head // 2) * 16 + (head % 2) * (chunks + 1)
+        for c in range(chunks):
+            place = (chunks - 1 - c) * 128
+            bias_out[head : head + 1, place : place + 128] = mirrored[base + c : base + c + 1, :]
+        bias_out[head : head + 1, chunks * 128 :] = mirrored[base + chunks : base + chunks + 1, :1]
+    for copy in copies:
+        copy.wait()
 
 
 def body(queries, keys, values, rel_bias, grad_out):
@@ -419,43 +497,44 @@
     ctxw = NB * frames
     own = GROUP * frames
     rows = own + 2 * ctxw
-    count = 2 * ctxw + 1
-    reversed_bias = jnp.pad(
-        rel_bias[:, ::-1], ((0, 0), (0, span - count)), constant_values=EXCLUDED
-    )
     block = jax.ShapeDtypeStruct(queries.shape, jnp.bfloat16)
     bf16, f32 = jnp.bfloat16, jnp.float32
     dma = pltpu.SemaphoreType.DMA
-    hbm = pl.BlockSpec(memory_space=pl.ANY)
+    anywhere = pl.BlockSpec(memory_space=pl.ANY)
+    hbm = pl.BlockSpec(memory_space=pltpu.HBM)
     vmem = pl.BlockSpec(memory_space=pltpu.VMEM)
     macs = 6 * GROUP * frames * span * 2 * PAIRS * HEAD
-    att, gq, gk, gv, bias = pl.pallas_call(
+    parts = pl.pallas_call(
         functools.partial(kernel, n_dp, n_groups, frames),
         out_shape=(block, block, block, block, jax.ShapeDtypeStruct((GROUP, PAIRS, 16, 128), f32)),
         in_specs=[hbm, hbm, hbm, hbm, vmem],
-        out_specs=(hbm, hbm, hbm, hbm, vmem),
+        out_specs=(anywhere, anywhere, anywhere, anywhere, vmem),
         scratch_shapes=[
             pltpu.VMEM((PAIRS, own, LANES), bf16),
             pltpu.VMEM((PAIRS, own, LANES), bf16),
             pltpu.VMEM((PAIRS, rows, LANES), bf16),
             pltpu.VMEM((PAIRS, rows, LANES), bf16),
+            pltpu.VMEM((HEADS, span), f32),
             pltpu.VMEM((PAIRS, 2 * frames, span), f32),
             pltpu.VMEM((PAIRS, 2 * frames, span), f32),
-            pltpu.VMEM((PAIRS, rows, LANES), f32),
-            pltpu.VMEM((PAIRS, rows, LANES), f32),
-            pltpu.VMEM((2, PAIRS, 2, ctxw, LANES), bf16),
-            pltpu.VMEM((2, PAIRS, 2, ctxw, LANES), bf16),
+            pltpu.VMEM((PAIRS, LANES, rows), f32),
+            pltpu.VMEM((PAIRS, LANES, rows), f32),
+            pltpu.VMEM((2, 2 * frames, span), bf16),
+            pltpu.VMEM((2, 2 * frames, span), bf16),
+            pltpu.VMEM((2, LANES, 2 * frames), bf16),
+            pltpu.VMEM((2, LANES, 2 * frames), bf16),
+            pltpu.VMEM((2, PAIRS, 2, NB, LANES, frames), bf16),
+            pltpu.VMEM((2, PAIRS, 2, NB, LANES, frames), bf16),
             pltpu.VMEM((4, PAIRS, GROUP, frames, LANES), bf16),
             pltpu.VMEM((n_peer, PAIRS, 16, 128), f32),
-            pltpu.VMEM((GROUP, PAIRS, 16, 128), f32),
             pltpu.VMEM((PAIRS, 16, 128), f32),
             dma((4, PAIRS)),
             dma((4, PAIRS, GROUP)),
             dma((4, PAIRS, GROUP)),
-            dma((2, PAIRS, 2)),
-            dma((2, PAIRS, 2)),
-            dma((2, PAIRS, 2)),
-            dma((2, PAIRS, 2)),
+            dma((2, PAIRS, 2, NB)),
+            dma((2, PAIRS, 2, NB)),
+            dma((2, PAIRS, 2, NB)),
+            dma((2, PAIRS, 2, NB)),
             dma((4, PAIRS, GROUP)),
             dma((4, PAIRS, GROUP)),
             dma((4, PAIRS)),
@@ -465,16 +544,23 @@
             dma((PAIRS, GROUP)),
         ],
         compiler_params=pltpu.CompilerParams(
-            collective_id=0, has_side_effects=True, vmem_limit_bytes=48 * 1024 * 1024
+            collective_id=0, has_side_effects=True, vmem_limit_bytes=VMEM_LIMIT
         ),
         cost_estimate=pl.CostEstimate(
             flops=2 * macs, bytes_accessed=8 * frames * width * 2, transcendentals=own * span * 2 * PAIRS
         ),
-    )(queries, keys, values, grad_out, reversed_bias)
-    tiles = 2 * (span // 128)
-    table = bias[:, :, :tiles, :].reshape(HEADS, span)
-    grad_bias = table[:, :count][:, ::-1]
-    return (att, gq, gk, gv, grad_bias)
+    )(queries, keys, values, grad_out, rel_bias)
+    return pl.pallas_call(
+        finish,
+        out_shape=(block, block, block, block, jax.ShapeDtypeStruct(rel_bias.shape, f32)),
+        in_specs=[anywhere, anywhere, anywhere, anywhere, vmem],
+        out_specs=(hbm, hbm, hbm, hbm, vmem),
+        scratch_shapes=[dma((4,))],
+        compiler_params=pltpu.CompilerParams(vmem_limit_bytes=VMEM_LIMIT),
+        cost_estimate=pl.CostEstimate(
+            flops=0, bytes_accessed=8 * frames * width * 2, transcendentals=0
+        ),
+    )(*parts)
 
 
 def solution(mesh):

time: 58.6 us -> 80.1 us (1.37)
  Pallas kernels: 47.5 us -> 79.2 us
  local copies, waits for them, and re-layouts: 10.1 us -> 0 us
    pallas_call x0 -> x1, Pallas kernels: none -> 34.4 us  [body(): pl.pallas_call(finish, out_shape=(block, block, block, block, jax.ShapeDt...]
    unnamed x16 -> x0, local copies, waits for them, and re-layouts: 10.1 us -> none
    pallas_call x1, Pallas kernels: 47.5 us -> 44.8 us  [body(): pl.pallas_call(functools.partial(kernel, n_dp, n_groups, frames), out_sha...]
where the time goes in v1:
time: 80.1 us; the launch traced here: 79.8 us
  Pallas kernels  79.2 us (99%)
    pallas_call x1, Pallas kernels, body(): pl.pallas_call(functools.partial(kernel, n_dp, n_groups, frames), out_sha...  44.8 us
    pallas_call x1, Pallas kernels, body(): pl.pallas_call(finish, out_shape=(block, block, block, block, jax.ShapeDt...  34.4 us

profile of v1, /device:TPU:0, one launch (start us, length us, event | category | flops | bytes accessed | tf_op | source)
XLA Modules:
  0.0 79.8 jit_solution(9365101304758641541)
XLA Ops:
  0.6 44.8 %shard_map.92 = (bf16[1,128,1024]{2,1,0:T(8,128)(2,1)}, bf16[1,128,1024]{2,1,0:T(8,128)(2,1)}, bf16[1,128,1024]{2,1,0:T(8,128)(2,1)}, bf16[1,128,1024]{2,1,0:T(8,128)(2,1)}, f32[4,2,16,128]{3,2,1,0:T(8,128)}) custom-call(bf16[1,128,1024]{2,1,0:T(8,128)(2,1)} %q_hbm.1, bf16[1,128,1024]{2,1,0:T(8,128)(2,1)} %k_hbm.1, bf16[1,128,1024]{2,1,0:T(8,128)(2,1)} %v_hbm.1, ...), custom_call_target="tpu_custom_call" | custom-call | flops 1409286144 | bytes 2097152 | tf_op jit(solution)/shard_map/pallas_call | solution.py:507
  45.5 34.4 %shard_map.93 = (bf16[1,128,1024]{2,1,0:T(8,128)(2,1)}, bf16[1,128,1024]{2,1,0:T(8,128)(2,1)}, bf16[1,128,1024]{2,1,0:T(8,128)(2,1)}, bf16[1,128,1024]{2,1,0:T(8,128)(2,1)}, f32[16,769]{1,0:T(8,128)}) custom-call(bf16[1,128,1024]{2,1,0:T(8,128)(2,1)} %get-tuple-element.10.att, bf16[1,128,1024]{2,1,0:T(8,128)(2,1)} %get-tuple-element.11.gq, ...), custom_call_target="tpu_custom_call" | custom-call | bytes 2097152 | tf_op jit(solution)/shard_map/pallas_call | solution.py:553

commit v2 on v1

v2 whole, which is shorter than its diff:
```python
import functools
import math

import jax
import jax.numpy as jnp
from jax import lax
from jax.experimental import pallas as pl
from jax.experimental.pallas import tpu as pltpu
from jax.sharding import PartitionSpec as P

HEADS = 16
HEAD = 64
NB = 3
GROUP = 4
PAIRS = HEADS // GROUP // 2
LANES = 2 * HEAD
EXCLUDED = -1e30
VMEM_LIMIT = 60 * 1024 * 1024
MESH = pl.DeviceIdType.MESH
Q, K, V, G = 0, 1, 2, 3
NT = (((1,), (1,)), ((), ()))


ORDER = (0, 3, 1, 2)
DONE = {0: ((0, 0),), 3: ((1, 2),), 1: ((0, 1),), 2: ((1, 0), (1, 1), (0, 2))}


def dot(a, b, dims=(((1,), (0,)), ((), ()))):
    return lax.dot_general(a, b, dims, preferred_element_type=jnp.float32)


def mirror_lanes(x):
    row = lax.broadcasted_iota(jnp.int32, (128, 128), 0)
    col = lax.broadcasted_iota(jnp.int32, (128, 128), 1)
    exchange = (row + col == 127).astype(jnp.float32)
    return jnp.dot(
        x, exchange, precision=lax.Precision.HIGHEST, preferred_element_type=jnp.float32
    )


def kernel(
    n_dp, n_groups, frames,
    q_hbm, k_hbm, v_hbm, g_hbm, rel_ref,
    parts_out, bias_out,
    qgbuf, kvbuf, rev_buf, bias_tab, bias_acc, gk_acc, gv_acc,
    ds_buf, w_buf, qt_buf, gt_buf, halo_out, halo_in, ostage, b1buf, sum_buf,
    loc_sem, a_send, kv_recv, qg_recv, h_send, h_recv, g_send, g_recv,
    o_send, o_recv, o_loc, b1_send, b1_recv, b2_send, b2_recv,
):
    span = (2 * NB + 1) * frames
    ctxw = NB * frames
    own = GROUP * frames
    score_scale = 1.0 / math.sqrt(HEAD)
    dp = lax.axis_index("dp")
    ctx = lax.axis_index("ctx")
    g = lax.div(ctx, GROUP)
    i = lax.rem(ctx, GROUP)
    n_peer = n_dp * n_groups
    slot = dp * n_groups + g
    has_lo = g > 0
    has_hi = g < n_groups - 1
    srcs = (q_hbm, k_hbm, v_hbm, g_hbm)
    accs = (gk_acc, gv_acc)

    def group_dev(j):
        return {"dp": dp, "ctx": g * GROUP + j}

    def side_dev(direction):
        return {"dp": dp, "ctx": ctx + (GROUP if direction else -GROUP)}

    def peer_dev(s):
        return {"dp": lax.div(s, n_groups), "ctx": lax.rem(s, n_groups) * GROUP + i}

    def lanes(j, p):
        return pl.ds(pl.multiple_of((j * PAIRS + p) * LANES, LANES), LANES)

    def rows_of(arr, p, j):
        if arr in (K, V):
            start = pl.multiple_of(ctxw + j * frames, frames)
            return kvbuf.at[p, arr - K, pl.ds(start, frames), :]
        start = pl.multiple_of(j * frames, frames)
        return qgbuf.at[p, 0 if arr == Q else 1, pl.ds(start, frames), :]

    def local_in(arr, p):
        return pltpu.make_async_copy(srcs[arr].at[0, :, lanes(i, p)], rows_of(arr, p, i), loc_sem.at[arr, p])

    def remote(src, dst, send_sem, recv_sem, device):
        return pltpu.make_async_remote_copy(
            src_ref=src, dst_ref=dst, send_sem=send_sem, recv_sem=recv_sem,
            device_id=device, device_id_type=MESH,
        )

    def a_copy(arr, p, j):
        recv = kv_recv.at[p, i] if arr in (K, V) else qg_recv.at[p]
        return remote(
            srcs[arr].at[0, :, lanes(j, p)], rows_of(arr, p, i), a_send.at[0], recv, group_dev(j)
        )

    def kv_arrival(p, j):
        block = kvbuf.at[p, :, pl.ds(pl.multiple_of(ctxw + j * frames, frames), frames), :]
        return remote(block, block, a_send.at[0], kv_recv.at[p, j], group_dev(j))

    def qg_arrival(p):
        blocks = qgbuf.at[p, :, pl.ds(0, own - frames), :]
        return remote(blocks, blocks, a_send.at[0], qg_recv.at[p], group_dev(i))

    def halo_copy(p, direction, j):
        src = pl.multiple_of(ctxw + j * frames, frames)
        place = j - 1 if direction else j
        dst = pl.multiple_of(place * frames + (0 if direction else ctxw + own), frames)
        return remote(
            kvbuf.at[p, :, pl.ds(src, frames), :],
            kvbuf.at[p, :, pl.ds(dst, frames), :],
            h_send.at[direction], h_recv.at[p, direction], side_dev(direction),
        )

    def halo_arrival(p, direction):
        blocks = kvbuf.at[p, :, pl.ds(0 if direction else ctxw + own, ctxw), :]
        return remote(
            blocks, blocks, h_send.at[direction], h_recv.at[p, direction], side_dev(direction)
        )

    def grad_copy(p, direction, blk):
        return remote(
            halo_out.at[p, direction, blk], halo_in.at[p, direction, blk],
            g_send.at[direction], g_recv.at[p, direction, blk], side_dev(direction),
        )

    def out_parts(half, p, j):
        return ostage.at[p, j, pl.ds(2 * half, 2)]

    def out_copy(half, p, j):
        return remote(
            out_parts(half, p, j), parts_out.at[pl.ds(2 * half, 2), :, lanes(i, p)],
            o_send.at[0], o_recv.at[0], group_dev(j),
        )

    def send_out(half, p, j):
        @pl.when(j != i)
        def _():
            out_copy(half, p, j).start()

        @pl.when(j == i)
        def _():
            pltpu.make_async_copy(
                out_parts(half, p, j), parts_out.at[pl.ds(2 * half, 2), :, lanes(i, p)], o_loc.at[0]
            ).start()

    def b1_copy(p, s):
        return remote(
            b1buf.at[p, slot], b1buf.at[p, slot], b1_send.at[0], b1_recv.at[p], peer_dev(s)
        )

    def b2_copy(p, j):
        return remote(sum_buf.at[p], bias_out.at[p, i], b2_send.at[0], b2_recv.at[p], group_dev(j))

    def others(fn):
        core = lax.rem(i, 2)
        far = 2 - 2 * lax.div(i, 2)
        fn(i + 1 - 2 * core)
        fn(far + core)
        fn(far + 1 - core)

    def all_peers(fn):
        def step(t, carry):
            fn(lax.rem(slot + t, n_peer))
            return carry

        lax.fori_loop(1, n_peer, step, 0)

    barrier = pltpu.get_barrier_semaphore()

    def greet(device):
        pl.semaphore_signal(barrier, inc=1, device_id=device, device_id_type=MESH)

    others(lambda j: greet(group_dev(j)))
    all_peers(lambda s: greet(peer_dev(s)))
    for p in range(PAIRS):
        for arr in (K, V, Q, G):
            local_in(arr, p).start()

    bias_acc[...] = jnp.zeros_like(bias_acc)
    gk_acc[...] = jnp.zeros_like(gk_acc)
    gv_acc[...] = jnp.zeros_like(gv_acc)
    edge_zero = jnp.zeros((PAIRS, 2, ctxw, LANES), jnp.bfloat16)
    edge_grad = jnp.zeros((PAIRS, NB, 2, LANES, frames), jnp.bfloat16)

    @pl.when(jnp.logical_not(has_lo))
    def _():
        kvbuf[:, :, :ctxw, :] = edge_zero
        halo_in[:, 1] = edge_grad

    @pl.when(jnp.logical_not(has_hi))
    def _():
        kvbuf[:, :, ctxw + own :, :] = edge_zero
        halo_in[:, 0] = edge_grad

    pl.semaphore_wait(barrier, GROUP - 1 + n_peer - 1)

    def send_inputs(p):
        for arr in (K, V, Q, G):
            others(lambda j: a_copy(arr, p, j).start())

    send_inputs(0)

    chunks = 2 * ctxw // 128
    for c in range(chunks):
        rev_buf[:, (chunks - 1 - c) * 128 : (chunks - c) * 128] = mirror_lanes(
            rel_ref[:, c * 128 : (c + 1) * 128]
        )
    last_lane = lax.broadcasted_iota(jnp.int32, (HEADS, 128), 1) == 127
    rev_buf[:, 2 * ctxw :] = jnp.where(
        last_lane, rel_ref[:, 2 * ctxw : 2 * ctxw + 1], jnp.float32(EXCLUDED)
    )
    for p in range(PAIRS):
        for h in range(2):
            row = rev_buf[pl.ds(i * (2 * PAIRS) + 2 * p + h, 1), :]
            table = jnp.broadcast_to(row, (frames, span))
            bias_tab[p, h * frames : (h + 1) * frames, :] = pltpu.roll(
                table, 1, 1, stride=1, stride_axis=0
            )
    def forward_halo(p):
        def forward(j):
            @pl.when(has_lo & (j < NB))
            def _():
                halo_copy(p, 0, j).start()

            @pl.when(has_hi & (j > 0))
            def _():
                halo_copy(p, 1, j).start()

        local_in(K, p).wait()
        local_in(V, p).wait()
        forward(i)

        def passed_on(j):
            kv_arrival(p, j).wait_recv()
            forward(j)

        others(passed_on)

    def wait_inputs(p):
        local_in(Q, p).wait()
        local_in(G, p).wait()
        qg_arrival(p).wait_recv()

        @pl.when(has_lo)
        def _():
            halo_arrival(p, 1).wait_recv()

        @pl.when(has_hi)
        def _():
            halo_arrival(p, 0).wait_recv()

    low = lax.broadcasted_iota(jnp.int32, (frames, LANES), 1) < HEAD

    def stack_heads(x):
        zero = jnp.zeros_like(x)
        return jnp.concatenate([jnp.where(low, x, zero), jnp.where(low, zero, x)], axis=0)

    def merge_heads(x):
        return jnp.where(low, x[:frames], x[frames:])

    column = lax.broadcasted_iota(jnp.int32, (1, span), 1)

    top_half = lax.broadcasted_iota(jnp.int32, (LANES, frames), 0) < HEAD

    def stack_turned(x):
        turned = x.T
        zero = jnp.zeros_like(turned)
        return jnp.concatenate(
            [jnp.where(top_half, turned, zero), jnp.where(top_half, zero, turned)], axis=1
        ).astype(jnp.bfloat16)

    def softmax_part(n, p, b):
        own_rows = slice(b * frames, (b + 1) * frames)
        window = slice(b * frames, b * frames + span)
        key_row = column + ((g * GROUP - NB + b) * frames)
        exists = (key_row >= 0) & (key_row < n_groups * own)
        edge = jnp.where(exists, 0.0, EXCLUDED).astype(jnp.float32)
        kw = kvbuf[p, 0, window, :]
        vw = kvbuf[p, 1, window, :]
        q32 = qgbuf[p, 0, own_rows, :].astype(jnp.float32) * score_scale
        g32 = qgbuf[p, 1, own_rows, :].astype(jnp.float32)
        qs = stack_heads(q32).astype(jnp.bfloat16)
        gs32 = stack_heads(g32)
        gs = gs32.astype(jnp.bfloat16)
        qt_buf[n % 2] = stack_turned(q32)
        gt_buf[n % 2] = stack_turned(g32)
        scores = dot(qs, kw, NT) + bias_tab[p] + edge
        top = jnp.max(scores, axis=1, keepdims=True)
        expd = jnp.exp(scores - top)
        total = jnp.sum(expd, axis=1, keepdims=True)
        probs = expd * (1.0 / total)
        weights = probs.astype(jnp.bfloat16)
        w_buf[n % 2] = weights
        attended = merge_heads(dot(weights, vw)).astype(jnp.bfloat16)
        ostage[p, b, 0] = attended
        wide = attended.astype(jnp.float32)
        delta = jnp.sum(gs32 * jnp.concatenate([wide, wide], axis=0), axis=1, keepdims=True)
        dscore = probs * (dot(gs, vw, NT) - delta)
        ds_buf[n % 2] = dscore.astype(jnp.bfloat16)
        bias_acc[p] += dscore

    def grad_part(n, p, b):
        window = slice(b * frames, b * frames + span)
        dscore_low = ds_buf[n % 2]
        grad_q = merge_heads(dot(dscore_low, kvbuf[p, 0, window, :])) * score_scale
        ostage[p, b, 1] = grad_q.astype(jnp.bfloat16)
        gk_acc[p, :, window] += dot(qt_buf[n % 2], dscore_low)
        gv_acc[p, :, window] += dot(gt_buf[n % 2], w_buf[n % 2])

    def send_grads(p, b):
        send_out(0, p, b)
        for direction, blk in DONE[b]:
            start = blk * frames + (ctxw + own if direction else 0)

            @pl.when(has_hi if direction else has_lo)
            def _():
                for a in range(2):
                    halo_out[p, direction, blk, a] = accs[a][p, :, start : start + frames].astype(
                        jnp.bfloat16
                    )
                grad_copy(p, direction, blk).start()

    def send_bias(p):
        sub = lax.broadcasted_iota(jnp.int32, (8, span), 0)
        b1buf[p, slot] = jnp.zeros((16, 128), jnp.float32)
        for h in range(2):
            part = bias_acc[p, h * frames : (h + 1) * frames, :]
            rows = frames
            while rows > 8:
                rows //= 2
                part = part[:rows] + pltpu.roll(part[rows:], span - rows, 1)
            for s in (4, 2, 1):
                part = jnp.where((sub & s) != 0, pltpu.roll(part, span - s, 1), part)
            diag = pltpu.roll(jnp.sum(part, axis=0, keepdims=True), span - 1, 1)
            for c in range(span // 128):
                n = h * (span // 128) + c
                b1buf[p, slot, n : n + 1, :] = diag[:, c * 128 : (c + 1) * 128]
        all_peers(lambda s: b1_copy(p, s).start())

    def sum_bias(p):
        others_part = b1buf.at[p, pl.ds(0, n_peer - 1)]
        remote(
            others_part, others_part, b1_send.at[0], b1_recv.at[p], group_dev(i)
        ).wait_recv()
        sum_buf[p] = lax.fori_loop(
            0, n_peer, lambda s, acc: acc + b1buf[p, s], jnp.zeros((16, 128), jnp.float32)
        )
        others(lambda j: b2_copy(p, j).start())
        bias_out[p, i] = sum_buf[p]

    def finish_grads(p):
        for j in (2, 0, 1, 3):
            if j < NB:
                @pl.when(has_lo)
                def _():
                    grad_copy(p, 1, j).wait_recv()
            if j > 0:
                @pl.when(has_hi)
                def _():
                    grad_copy(p, 0, j - 1).wait_recv()
            start = ctxw + j * frames
            for a in range(2):
                full = accs[a][p, :, start : start + frames]
                if j < NB:
                    full = full + halo_in[p, 1, j, a].astype(jnp.float32)
                if j > 0:
                    full = full + halo_in[p, 0, j - 1, a].astype(jnp.float32)
                ostage[p, j, 2 + a] = full.T.astype(jnp.bfloat16)
            send_out(1, p, j)

    units = [(p, b) for p in range(PAIRS) for b in ORDER]
    forward_halo(0)
    for p in range(1, PAIRS):
        send_inputs(p)
    for n, (p, b) in enumerate(units):
        if b == ORDER[0]:
            wait_inputs(p)
        softmax_part(n, p, b)
        if n > 0:
            grad_part(n - 1, *units[n - 1])
            send_grads(*units[n - 1])
        if b == ORDER[0]:
            if p + 1 < PAIRS:
                forward_halo(p + 1)
            if p > 0:
                send_bias(p - 1)
        if b == ORDER[2] and p > 0:
            sum_bias(p - 1)
            finish_grads(p - 1)
    send_bias(PAIRS - 1)
    grad_part(len(units) - 1, *units[-1])
    send_grads(*units[-1])
    sum_bias(PAIRS - 1)
    finish_grads(PAIRS - 1)

    def drain_send(ref, sem):
        remote(ref, ref, sem, sem, group_dev(i)).wait_send()

    def drain_recv(ref, sem):
        remote(ref, ref, sem, sem, group_dev(i)).wait_recv()

    for p in range(PAIRS):
        drain_recv(bias_out.at[p, pl.ds(0, GROUP - 1)], b2_recv.at[p])
    mine = PAIRS * LANES
    drain_recv(parts_out.at[:, :, pl.ds(0, (GROUP - 1) * mine)], o_recv.at[0])
    own_part = parts_out.at[:, :, pl.ds(0, mine)]
    pltpu.make_async_copy(own_part, own_part, o_loc.at[0]).wait()
    drain_send(parts_out.at[:, :, pl.ds(0, (GROUP - 1) * mine)], o_send.at[0])
    drain_send(parts_out.at[:, :, pl.ds(0, (GROUP - 1) * mine)], a_send.at[0])
    for direction, exists in ((0, has_lo), (1, has_hi)):
        @pl.when(exists)
        def _():
            drain_send(kvbuf.at[:, :, pl.ds(0, ctxw), :], h_send.at[direction])
            drain_send(halo_out.at[:, direction], g_send.at[direction])

    drain_send(b1buf.at[:, pl.ds(0, n_peer - 1)], b1_send.at[0])
    drain_send(bias_out.at[:, pl.ds(0, GROUP - 1)], b2_send.at[0])


def finish(parts, bias, att_out, gq_out, gk_out, gv_out, bias_out, held, in_sems, out_sems):
    outs = (att_out, gq_out, gk_out, gv_out)
    arrive = [pltpu.make_async_copy(parts.at[n], held.at[n], in_sems.at[n]) for n in range(4)]
    leave = [pltpu.make_async_copy(held.at[n], outs[n].at[0], out_sems.at[n]) for n in range(4)]
    for copy in arrive:
        copy.start()
    for n in range(4):
        arrive[n].wait()
        leave[n].start()
    chunks = bias_out.shape[1] // 128
    mirrored = mirror_lanes(bias[...].reshape(PAIRS * GROUP * 16, 128))
    for head in range(HEADS):
        dev, pair, odd = head // (2 * PAIRS), head // 2 % PAIRS, head % 2
        base = (pair * GROUP + dev) * 16 + odd * (chunks + 1)
        for c in range(chunks):
            place = (chunks - 1 - c) * 128
            bias_out[head : head + 1, place : place + 128] = mirrored[base + c : base + c + 1, :]
        bias_out[head : head + 1, chunks * 128 :] = mirrored[base + chunks : base + chunks + 1, :1]
    for copy in leave:
        copy.wait()


def body(queries, keys, values, rel_bias, grad_out):
    rec_dev, frames, width = queries.shape
    n_dp = lax.axis_size("dp")
    n_groups = lax.axis_size("ctx") // GROUP
    n_peer = n_dp * n_groups
    span = (2 * NB + 1) * frames
    ctxw = NB * frames
    own = GROUP * frames
    rows = own + 2 * ctxw
    block = jax.ShapeDtypeStruct(queries.shape, jnp.bfloat16)
    bf16, f32 = jnp.bfloat16, jnp.float32
    dma = pltpu.SemaphoreType.DMA
    anywhere = pl.BlockSpec(memory_space=pl.ANY)
    hbm = pl.BlockSpec(memory_space=pltpu.HBM)
    vmem = pl.BlockSpec(memory_space=pltpu.VMEM)
    macs = 6 * GROUP * frames * span * 2 * PAIRS * HEAD
    parts, bias = pl.pallas_call(
        functools.partial(kernel, n_dp, n_groups, frames),
        out_shape=(
            jax.ShapeDtypeStruct((4, frames, width), bf16),
            jax.ShapeDtypeStruct((PAIRS, GROUP, 16, 128), f32),
        ),
        in_specs=[hbm, hbm, hbm, hbm, vmem],
        out_specs=(anywhere, vmem),
        scratch_shapes=[
            pltpu.VMEM((PAIRS, 2, own, LANES), bf16),
            pltpu.VMEM((PAIRS, 2, rows, LANES), bf16),
            pltpu.VMEM((HEADS, span), f32),
            pltpu.VMEM((PAIRS, 2 * frames, span), f32),
            pltpu.VMEM((PAIRS, 2 * frames, span), f32),
            pltpu.VMEM((PAIRS, LANES, rows), f32),
            pltpu.VMEM((PAIRS, LANES, rows), f32),
            pltpu.VMEM((2, 2 * frames, span), bf16),
            pltpu.VMEM((2, 2 * frames, span), bf16),
            pltpu.VMEM((2, LANES, 2 * frames), bf16),
            pltpu.VMEM((2, LANES, 2 * frames), bf16),
            pltpu.VMEM((PAIRS, 2, NB, 2, LANES, frames), bf16),
            pltpu.VMEM((PAIRS, 2, NB, 2, LANES, frames), bf16),
            pltpu.VMEM((PAIRS, GROUP, 4, frames, LANES), bf16),
            pltpu.VMEM((PAIRS, n_peer, 16, 128), f32),
            pltpu.VMEM((PAIRS, 16, 128), f32),
            dma((4, PAIRS)),
            dma((1,)),
            dma((PAIRS, GROUP)),
            dma((PAIRS,)),
            dma((2,)),
            dma((PAIRS, 2)),
            dma((2,)),
            dma((PAIRS, 2, NB)),
            dma((1,)),
            dma((1,)),
            dma((1,)),
            dma((1,)),
            dma((PAIRS,)),
            dma((1,)),
            dma((PAIRS,)),
        ],
        compiler_params=pltpu.CompilerParams(
            collective_id=0, has_side_effects=True, vmem_limit_bytes=VMEM_LIMIT
        ),
        cost_estimate=pl.CostEstimate(
            flops=2 * macs, bytes_accessed=8 * frames * width * 2, transcendentals=own * span * 2 * PAIRS
        ),
    )(queries, keys, values, grad_out, rel_bias)
    return pl.pallas_call(
        finish,
        out_shape=(block, block, block, block, jax.ShapeDtypeStruct(rel_bias.shape, f32)),
        in_specs=[anywhere, vmem],
        out_specs=(hbm, hbm, hbm, hbm, vmem),
        scratch_shapes=[pltpu.VMEM((4, frames, width), bf16), dma((4,)), dma((4,))],
        compiler_params=pltpu.CompilerParams(vmem_limit_bytes=VMEM_LIMIT),
        cost_estimate=pl.CostEstimate(
            flops=0, bytes_accessed=8 * frames * width * 2, transcendentals=0
        ),
    )(parts, bias)


def solution(mesh):
    placed = (
        P("dp", "ctx", None),
        P("dp", "ctx", None),
        P("dp", "ctx", None),
        P(),
        P("dp", "ctx", None),
    )
    return jax.shard_map(
        body,
        mesh=mesh,
        in_specs=placed,
        out_specs=(
            P("dp", "ctx", None),
            P("dp", "ctx", None),
            P("dp", "ctx", None),
            P("dp", "ctx", None),
            P(),
        ),
        check_vma=False,
    )
```

time: 80.1 us -> 47 us (0.59)
  Pallas kernels: 79.2 us -> 46.1 us
    pallas_call x1, Pallas kernels: 34.4 us -> 3.44 us  [body(): pl.pallas_call(finish, out_shape=(block, block, block, block, jax.ShapeDt...]
    pallas_call x1, Pallas kernels: 44.8 us -> 42.6 us  [body(): pl.pallas_call(functools.partial(kernel, n_dp, n_groups, frames), out_sha...]
where the time goes in v2:
time: 47 us; the launch traced here: 46.7 us
  Pallas kernels  46.1 us (98%)
  between operations  0.64 us (1%)
    pallas_call x1, Pallas kernels, body(): pl.pallas_call(functools.partial(kernel, n_dp, n_groups, frames), out_sha...  42.6 us
    pallas_call x1, Pallas kernels, body(): pl.pallas_call(finish, out_shape=(block, block, block, block, jax.ShapeDt...  3.44 us

profile of v2, /device:TPU:0, one launch (start us, length us, event | category | flops | bytes accessed | tf_op | source)
XLA Modules:
  0.0 46.7 jit_solution(1676105300309162781)
XLA Ops:
  0.6 42.6 %shard_map.92 = (bf16[4,128,1024]{2,1,0:T(8,128)(2,1)}, f32[2,4,16,128]{3,2,1,0:T(8,128)}) custom-call(bf16[1,128,1024]{2,1,0:T(8,128)(2,1)} %q_hbm.1, bf16[1,128,1024]{2,1,0:T(8,128)(2,1)} %k_hbm.1, bf16[1,128,1024]{2,1,0:T(8,128)(2,1)} %v_hbm.1, bf16[1,128,1024]{2,1,0:T(8,128)(2,1)} %g_hbm.1, f32[16,769]{1,0:T(8,128)} %rel_ref.1), custom_call_target="tpu_custom_call" | custom-call | flops 1409286144 | bytes 2097152 | tf_op jit(solution)/shard_map/pallas_call | solution.py:461
  43.3 3.4 %shard_map.93 = (bf16[1,128,1024]{2,1,0:T(8,128)(2,1)}, bf16[1,128,1024]{2,1,0:T(8,128)(2,1)}, bf16[1,128,1024]{2,1,0:T(8,128)(2,1)}, bf16[1,128,1024]{2,1,0:T(8,128)(2,1)}, f32[16,769]{1,0:T(8,128)}) custom-call(bf16[4,128,1024]{2,1,0:T(8,128)(2,1)} %get-tuple-element.7.parts, f32[2,4,16,128]{3,2,1,0:T(8,128)} %get-tuple-element.8.bias), custom_call_target="tpu_custom_call" | custom-call | bytes 2097152 | tf_op jit(solution)/shard_map/pallas_call | solution.py:509

commit v3 on v2

--- a/solution.py
+++ b/solution.py
@@ -15,7 +15,7 @@
 PAIRS = HEADS // GROUP // 2
 LANES = 2 * HEAD
 EXCLUDED = -1e30
-VMEM_LIMIT = 60 * 1024 * 1024
+VMEM_LIMIT = 40 * 1024 * 1024
 MESH = pl.DeviceIdType.MESH
 Q, K, V, G = 0, 1, 2, 3
 NT = (((1,), (1,)), ((), ()))
@@ -40,9 +40,9 @@
 
 def kernel(
     n_dp, n_groups, frames,
-    q_hbm, k_hbm, v_hbm, g_hbm, rel_ref,
+    q_hbm, k_hbm, v_hbm, g_hbm, rel_hbm,
     parts_out, bias_out,
-    qgbuf, kvbuf, rev_buf, bias_tab, bias_acc, gk_acc, gv_acc,
+    inbuf, rel_ref, qgbuf, kvbuf, rev_buf, bias_tab, bias_acc, gk_acc, gv_acc,
     ds_buf, w_buf, qt_buf, gt_buf, halo_out, halo_in, ostage, b1buf, sum_buf,
     loc_sem, a_send, kv_recv, qg_recv, h_send, h_recv, g_send, g_recv,
     o_send, o_recv, o_loc, b1_send, b1_recv, b2_send, b2_recv,
@@ -81,8 +81,11 @@
         start = pl.multiple_of(j * frames, frames)
         return qgbuf.at[p, 0 if arr == Q else 1, pl.ds(start, frames), :]
 
-    def local_in(arr, p):
-        return pltpu.make_async_copy(srcs[arr].at[0, :, lanes(i, p)], rows_of(arr, p, i), loc_sem.at[arr, p])
+    def load(arr):
+        return pltpu.make_async_copy(srcs[arr].at[0], inbuf.at[arr], loc_sem.at[arr])
+
+    def place_own(arr, p):
+        rows_of(arr, p, i)[...] = inbuf[arr, :, lanes(i, p)]
 
     def remote(src, dst, send_sem, recv_sem, device):
         return pltpu.make_async_remote_copy(
@@ -93,7 +96,7 @@
     def a_copy(arr, p, j):
         recv = kv_recv.at[p, i] if arr in (K, V) else qg_recv.at[p]
         return remote(
-            srcs[arr].at[0, :, lanes(j, p)], rows_of(arr, p, i), a_send.at[0], recv, group_dev(j)
+            inbuf.at[arr, :, lanes(j, p)], rows_of(arr, p, i), a_send.at[0], recv, group_dev(j)
         )
 
     def kv_arrival(p, j):
@@ -175,9 +178,10 @@
 
     others(lambda j: greet(group_dev(j)))
     all_peers(lambda s: greet(peer_dev(s)))
-    for p in range(PAIRS):
-        for arr in (K, V, Q, G):
-            local_in(arr, p).start()
+    load_rel = pltpu.make_async_copy(rel_hbm, rel_ref, loc_sem.at[4])
+    for arr in (K, V, Q, G):
+        load(arr).start()
+    load_rel.start()
 
     bias_acc[...] = jnp.zeros_like(bias_acc)
     gk_acc[...] = jnp.zeros_like(gk_acc)
@@ -201,7 +205,13 @@
         for arr in (K, V, Q, G):
             others(lambda j: a_copy(arr, p, j).start())
 
+    for arr in (K, V, Q, G):
+        load(arr).wait()
     send_inputs(0)
+    for arr in (K, V, Q, G):
+        for p in range(PAIRS):
+            place_own(arr, p)
+    load_rel.wait()
 
     chunks = 2 * ctxw // 128
     for c in range(chunks):
@@ -229,8 +239,6 @@
             def _():
                 halo_copy(p, 1, j).start()
 
-        local_in(K, p).wait()
-        local_in(V, p).wait()
         forward(i)
 
         def passed_on(j):
@@ -240,8 +248,6 @@
         others(passed_on)
 
     def wait_inputs(p):
-        local_in(Q, p).wait()
-        local_in(G, p).wait()
         qg_arrival(p).wait_recv()
 
         @pl.when(has_lo)
@@ -390,11 +396,11 @@
         if b == ORDER[2] and p > 0:
             sum_bias(p - 1)
             finish_grads(p - 1)
-    send_bias(PAIRS - 1)
     grad_part(len(units) - 1, *units[-1])
     send_grads(*units[-1])
+    send_bias(PAIRS - 1)
+    finish_grads(PAIRS - 1)
     sum_bias(PAIRS - 1)
-    finish_grads(PAIRS - 1)
 
     def drain_send(ref, sem):
         remote(ref, ref, sem, sem, group_dev(i)).wait_send()
@@ -420,15 +426,11 @@
     drain_send(bias_out.at[:, pl.ds(0, GROUP - 1)], b2_send.at[0])
 
 
-def finish(parts, bias, att_out, gq_out, gk_out, gv_out, bias_out, held, in_sems, out_sems):
+def finish(parts, bias, att_out, gq_out, gk_out, gv_out, bias_out, sems):
     outs = (att_out, gq_out, gk_out, gv_out)
-    arrive = [pltpu.make_async_copy(parts.at[n], held.at[n], in_sems.at[n]) for n in range(4)]
-    leave = [pltpu.make_async_copy(held.at[n], outs[n].at[0], out_sems.at[n]) for n in range(4)]
-    for copy in arrive:
+    leave = [pltpu.make_async_copy(parts.at[n], outs[n].at[0], sems.at[n]) for n in range(4)]
+    for copy in leave:
         copy.start()
-    for n in range(4):
-        arrive[n].wait()
-        leave[n].start()
     chunks = bias_out.shape[1] // 128
     mirrored = mirror_lanes(bias[...].reshape(PAIRS * GROUP * 16, 128))
     for head in range(HEADS):
@@ -458,15 +460,18 @@
     hbm = pl.BlockSpec(memory_space=pltpu.HBM)
     vmem = pl.BlockSpec(memory_space=pltpu.VMEM)
     macs = 6 * GROUP * frames * span * 2 * PAIRS * HEAD
+    operands = (queries, keys, values, grad_out, rel_bias)
     parts, bias = pl.pallas_call(
         functools.partial(kernel, n_dp, n_groups, frames),
         out_shape=(
             jax.ShapeDtypeStruct((4, frames, width), bf16),
             jax.ShapeDtypeStruct((PAIRS, GROUP, 16, 128), f32),
         ),
-        in_specs=[hbm, hbm, hbm, hbm, vmem],
+        in_specs=[hbm, hbm, hbm, hbm, hbm],
         out_specs=(anywhere, vmem),
         scratch_shapes=[
+            pltpu.VMEM((4, frames, width), bf16),
+            pltpu.VMEM(rel_bias.shape, f32),
             pltpu.VMEM((PAIRS, 2, own, LANES), bf16),
             pltpu.VMEM((PAIRS, 2, rows, LANES), bf16),
             pltpu.VMEM((HEADS, span), f32),
@@ -483,7 +488,7 @@
             pltpu.VMEM((PAIRS, GROUP, 4, frames, LANES), bf16),
             pltpu.VMEM((PAIRS, n_peer, 16, 128), f32),
             pltpu.VMEM((PAIRS, 16, 128), f32),
-            dma((4, PAIRS)),
+            dma((5,)),
             dma((1,)),
             dma((PAIRS, GROUP)),
             dma((PAIRS,)),
@@ -505,13 +510,13 @@
         cost_estimate=pl.CostEstimate(
             flops=2 * macs, bytes_accessed=8 * frames * width * 2, transcendentals=own * span * 2 * PAIRS
         ),
-    )(queries, keys, values, grad_out, rel_bias)
+    )(*(pltpu.with_memory_space_constraint(x, pltpu.HBM) for x in operands))
     return pl.pallas_call(
         finish,
         out_shape=(block, block, block, block, jax.ShapeDtypeStruct(rel_bias.shape, f32)),
-        in_specs=[anywhere, vmem],
+        in_specs=[vmem, vmem],
         out_specs=(hbm, hbm, hbm, hbm, vmem),
-        scratch_shapes=[pltpu.VMEM((4, frames, width), bf16), dma((4,)), dma((4,))],
+        scratch_shapes=[dma((4,))],
         compiler_params=pltpu.CompilerParams(vmem_limit_bytes=VMEM_LIMIT),
         cost_estimate=pl.CostEstimate(
             flops=0, bytes_accessed=8 * frames * width * 2, transcendentals=0

time: 47 us -> 42.8 us (0.911)
  Pallas kernels: 46.1 us -> 42 us
    pallas_call x1, Pallas kernels: 42.6 us -> 40.4 us  [body(): pl.pallas_call(functools.partial(kernel, n_dp, n_groups, frames), out_sha...]
    pallas_call x1, Pallas kernels: 3.44 us -> 1.62 us  [body(): pl.pallas_call(finish, out_shape=(block, block, block, block, jax.ShapeDt...]
where the time goes in v3:
time: 42.8 us; the launch traced here: 42.6 us
  Pallas kernels  42 us (98%)
  between operations  0.64 us (1%)
    pallas_call x1, Pallas kernels, body(): pl.pallas_call(functools.partial(kernel, n_dp, n_groups, frames), out_sha...  40.4 us
    pallas_call x1, Pallas kernels, body(): pl.pallas_call(finish, out_shape=(block, block, block, block, jax.ShapeDt...  1.62 us

profile of v3, /device:TPU:0, one launch (start us, length us, event | category | flops | bytes accessed | tf_op | source)
XLA Modules:
  0.0 42.6 jit_solution(7741242532854545831)
XLA Ops:
  0.6 40.4 %shard_map.92 = (bf16[4,128,1024]{2,1,0:T(8,128)(2,1)S(1)}, f32[2,4,16,128]{3,2,1,0:T(8,128)S(1)}) custom-call(bf16[1,128,1024]{2,1,0:T(8,128)(2,1)} %q_hbm.1, bf16[1,128,1024]{2,1,0:T(8,128)(2,1)} %k_hbm.1, bf16[1,128,1024]{2,1,0:T(8,128)(2,1)} %v_hbm.1, bf16[1,128,1024]{2,1,0:T(8,128)(2,1)} %g_hbm.1, f32[16,769]{1,0:T(8,128)} %rel_hbm.1), custom_call_target="tpu_custom_call" | custom-call | flops 1409286144 | bytes 2097152 | tf_op jit(solution)/shard_map/pallas_call | solution.py:464
  41.0 1.6 %shard_map.93 = (bf16[1,128,1024]{2,1,0:T(8,128)(2,1)}, bf16[1,128,1024]{2,1,0:T(8,128)(2,1)}, bf16[1,128,1024]{2,1,0:T(8,128)(2,1)}, bf16[1,128,1024]{2,1,0:T(8,128)(2,1)}, f32[16,769]{1,0:T(8,128)}) custom-call(bf16[4,128,1024]{2,1,0:T(8,128)(2,1)S(1)} %get-tuple-element.7.parts, f32[2,4,16,128]{3,2,1,0:T(8,128)S(1)} %get-tuple-element.8.bias), custom_call_target="tpu_custom_call" | custom-call | bytes 2097152 | tf_op jit(solution)/shard_map/pallas_call | solution.py:514

commit v4 on v3

--- a/solution.py
+++ b/solution.py
@@ -18,6 +18,7 @@
 VMEM_LIMIT = 40 * 1024 * 1024
 MESH = pl.DeviceIdType.MESH
 Q, K, V, G = 0, 1, 2, 3
+STRIP = 16
 NT = (((1,), (1,)), ((), ()))
 
 
@@ -43,7 +44,7 @@
     q_hbm, k_hbm, v_hbm, g_hbm, rel_hbm,
     parts_out, bias_out,
     inbuf, rel_ref, qgbuf, kvbuf, rev_buf, bias_tab, bias_acc, gk_acc, gv_acc,
-    ds_buf, w_buf, qt_buf, gt_buf, halo_out, halo_in, ostage, b1buf, sum_buf,
+    score_buf, prob_buf, dprob_buf, ds_buf, w_buf, qt_buf, gt_buf, halo_out, halo_in, ostage, b1buf, sum_buf,
     loc_sem, a_send, kv_recv, qg_recv, h_send, h_recv, g_send, g_recv,
     o_send, o_recv, o_loc, b1_send, b1_recv, b2_send, b2_recv,
 ):
@@ -293,20 +294,28 @@
         gs = gs32.astype(jnp.bfloat16)
         qt_buf[n % 2] = stack_turned(q32)
         gt_buf[n % 2] = stack_turned(g32)
-        scores = dot(qs, kw, NT) + bias_tab[p] + edge
-        top = jnp.max(scores, axis=1, keepdims=True)
-        expd = jnp.exp(scores - top)
-        total = jnp.sum(expd, axis=1, keepdims=True)
-        probs = expd * (1.0 / total)
-        weights = probs.astype(jnp.bfloat16)
-        w_buf[n % 2] = weights
+        m = n % 2
+        score_buf[m] = dot(qs, kw, NT)
+        dprob_buf[m] = dot(gs, vw, NT)
+        for r in range(0, 2 * frames, STRIP):
+            strip = slice(r, r + STRIP)
+            scores = score_buf[m, strip, :] + bias_tab[p, strip, :] + edge
+            top = jnp.max(scores, axis=1, keepdims=True)
+            expd = jnp.exp(scores - top)
+            total = jnp.sum(expd, axis=1, keepdims=True)
+            probs = expd * (1.0 / total)
+            prob_buf[m, strip, :] = probs
+            w_buf[m, strip, :] = probs.astype(jnp.bfloat16)
+        weights = w_buf[m]
         attended = merge_heads(dot(weights, vw)).astype(jnp.bfloat16)
         ostage[p, b, 0] = attended
         wide = attended.astype(jnp.float32)
         delta = jnp.sum(gs32 * jnp.concatenate([wide, wide], axis=0), axis=1, keepdims=True)
-        dscore = probs * (dot(gs, vw, NT) - delta)
-        ds_buf[n % 2] = dscore.astype(jnp.bfloat16)
-        bias_acc[p] += dscore
+        for r in range(0, 2 * frames, STRIP):
+            strip = slice(r, r + STRIP)
+            dscore = prob_buf[m, strip, :] * (dprob_buf[m, strip, :] - delta[strip])
+            ds_buf[m, strip, :] = dscore.astype(jnp.bfloat16)
+            bias_acc[p, strip, :] += dscore
 
     def grad_part(n, p, b):
         window = slice(b * frames, b * frames + span)
@@ -479,6 +488,9 @@
             pltpu.VMEM((PAIRS, 2 * frames, span), f32),
             pltpu.VMEM((PAIRS, LANES, rows), f32),
             pltpu.VMEM((PAIRS, LANES, rows), f32),
+            pltpu.VMEM((2, 2 * frames, span), f32),
+            pltpu.VMEM((2, 2 * frames, span), f32),
+            pltpu.VMEM((2, 2 * frames, span), f32),
             pltpu.VMEM((2, 2 * frames, span), bf16),
             pltpu.VMEM((2, 2 * frames, span), bf16),
             pltpu.VMEM((2, LANES, 2 * frames), bf16),

time: 42.8 us -> 42.7 us (level)
  no operation moved by 1% of the time
where the time goes in v4:
time: 42.7 us; the launch traced here: 42.5 us
  Pallas kernels  41.9 us (98%)
  between operations  0.64 us (1%)
    pallas_call x1, Pallas kernels, body(): pl.pallas_call(functools.partial(kernel, n_dp, n_groups, frames), out_sha...  40.3 us
    pallas_call x1, Pallas kernels, body(): pl.pallas_call(finish, out_shape=(block, block, block, block, jax.ShapeDt...  1.62 us

profile of v4, /device:TPU:0, one launch (start us, length us, event | category | flops | bytes accessed | tf_op | source)
XLA Modules:
  0.0 42.5 jit_solution(7767317919501823392)
XLA Ops:
  0.6 40.3 %shard_map.92 = (bf16[4,128,1024]{2,1,0:T(8,128)(2,1)S(1)}, f32[2,4,16,128]{3,2,1,0:T(8,128)S(1)}) custom-call(bf16[1,128,1024]{2,1,0:T(8,128)(2,1)} %q_hbm.1, bf16[1,128,1024]{2,1,0:T(8,128)(2,1)} %k_hbm.1, bf16[1,128,1024]{2,1,0:T(8,128)(2,1)} %v_hbm.1, bf16[1,128,1024]{2,1,0:T(8,128)(2,1)} %g_hbm.1, f32[16,769]{1,0:T(8,128)} %rel_hbm.1), custom_call_target="tpu_custom_call" | custom-call | flops 1409286144 | bytes 2097152 | tf_op jit(solution)/shard_map/pallas_call | solution.py:473
  40.9 1.6 %shard_map.93 = (bf16[1,128,1024]{2,1,0:T(8,128)(2,1)}, bf16[1,128,1024]{2,1,0:T(8,128)(2,1)}, bf16[1,128,1024]{2,1,0:T(8,128)(2,1)}, bf16[1,128,1024]{2,1,0:T(8,128)(2,1)}, f32[16,769]{1,0:T(8,128)}) custom-call(bf16[4,128,1024]{2,1,0:T(8,128)(2,1)S(1)} %get-tuple-element.7.parts, f32[2,4,16,128]{3,2,1,0:T(8,128)S(1)} %get-tuple-element.8.bias), custom_call_target="tpu_custom_call" | custom-call | bytes 2097152 | tf_op jit(solution)/shard_map/pallas_call | solution.py:526

commit v5 on v4

--- a/solution.py
+++ b/solution.py
@@ -17,7 +17,7 @@
 EXCLUDED = -1e30
 VMEM_LIMIT = 40 * 1024 * 1024
 MESH = pl.DeviceIdType.MESH
-Q, K, V, G = 0, 1, 2, 3
+K, V, Q, G = 0, 1, 2, 3
 STRIP = 16
 NT = (((1,), (1,)), ((), ()))
 
@@ -60,7 +60,7 @@
     slot = dp * n_groups + g
     has_lo = g > 0
     has_hi = g < n_groups - 1
-    srcs = (q_hbm, k_hbm, v_hbm, g_hbm)
+    srcs = (k_hbm, v_hbm, q_hbm, g_hbm)
     accs = (gk_acc, gv_acc)
 
     def group_dev(j):
@@ -72,21 +72,21 @@
     def peer_dev(s):
         return {"dp": lax.div(s, n_groups), "ctx": lax.rem(s, n_groups) * GROUP + i}
 
-    def lanes(j, p):
-        return pl.ds(pl.multiple_of((j * PAIRS + p) * LANES, LANES), LANES)
-
-    def rows_of(arr, p, j):
-        if arr in (K, V):
-            start = pl.multiple_of(ctxw + j * frames, frames)
-            return kvbuf.at[p, arr - K, pl.ds(start, frames), :]
-        start = pl.multiple_of(j * frames, frames)
-        return qgbuf.at[p, 0 if arr == Q else 1, pl.ds(start, frames), :]
-
-    def load(arr):
-        return pltpu.make_async_copy(srcs[arr].at[0], inbuf.at[arr], loc_sem.at[arr])
-
-    def place_own(arr, p):
-        rows_of(arr, p, i)[...] = inbuf[arr, :, lanes(i, p)]
+    def tile(j, p):
+        return j * PAIRS + p
+
+    def pair_rows(half, p, j):
+        if half == 0:
+            return kvbuf.at[p, :, pl.ds(pl.multiple_of(ctxw + j * frames, frames), frames), :]
+        return qgbuf.at[p, :, pl.ds(pl.multiple_of(j * frames, frames), frames), :]
+
+    def load(arr, t):
+        return pltpu.make_async_copy(
+            srcs[arr].at[0, :, t * LANES : (t + 1) * LANES], inbuf.at[t, arr], loc_sem.at[0]
+        )
+
+    def place_own(half, p):
+        pair_rows(half, p, i)[...] = inbuf[tile(i, p), 2 * half : 2 * half + 2]
 
     def remote(src, dst, send_sem, recv_sem, device):
         return pltpu.make_async_remote_copy(
@@ -94,10 +94,11 @@
             device_id=device, device_id_type=MESH,
         )
 
-    def a_copy(arr, p, j):
-        recv = kv_recv.at[p, i] if arr in (K, V) else qg_recv.at[p]
+    def a_copy(half, p, j):
+        recv = qg_recv.at[p] if half else kv_recv.at[p, i]
         return remote(
-            inbuf.at[arr, :, lanes(j, p)], rows_of(arr, p, i), a_send.at[0], recv, group_dev(j)
+            inbuf.at[tile(j, p), pl.ds(2 * half, 2)], pair_rows(half, p, i),
+            a_send.at[0], recv, group_dev(j),
         )
 
     def kv_arrival(p, j):
@@ -135,7 +136,7 @@
 
     def out_copy(half, p, j):
         return remote(
-            out_parts(half, p, j), parts_out.at[pl.ds(2 * half, 2), :, lanes(i, p)],
+            out_parts(half, p, j), parts_out.at[tile(i, p), pl.ds(2 * half, 2)],
             o_send.at[0], o_recv.at[0], group_dev(j),
         )
 
@@ -147,7 +148,7 @@
         @pl.when(j == i)
         def _():
             pltpu.make_async_copy(
-                out_parts(half, p, j), parts_out.at[pl.ds(2 * half, 2), :, lanes(i, p)], o_loc.at[0]
+                out_parts(half, p, j), parts_out.at[tile(i, p), pl.ds(2 * half, 2)], o_loc.at[0]
             ).start()
 
     def b1_copy(p, s):
@@ -179,9 +180,10 @@
 
     others(lambda j: greet(group_dev(j)))
     all_peers(lambda s: greet(peer_dev(s)))
-    load_rel = pltpu.make_async_copy(rel_hbm, rel_ref, loc_sem.at[4])
-    for arr in (K, V, Q, G):
-        load(arr).start()
+    load_rel = pltpu.make_async_copy(rel_hbm, rel_ref, loc_sem.at[1])
+    for t in range(GROUP * PAIRS):
+        for arr in (K, V, Q, G):
+            load(arr, t).start()
     load_rel.start()
 
     bias_acc[...] = jnp.zeros_like(bias_acc)
@@ -203,15 +205,14 @@
     pl.semaphore_wait(barrier, GROUP - 1 + n_peer - 1)
 
     def send_inputs(p):
-        for arr in (K, V, Q, G):
-            others(lambda j: a_copy(arr, p, j).start())
-
-    for arr in (K, V, Q, G):
-        load(arr).wait()
+        for half in range(2):
+            others(lambda j: a_copy(half, p, j).start())
+
+    pltpu.make_async_copy(inbuf, inbuf, loc_sem.at[0]).wait()
     send_inputs(0)
-    for arr in (K, V, Q, G):
-        for p in range(PAIRS):
-            place_own(arr, p)
+    for p in range(PAIRS):
+        for half in range(2):
+            place_own(half, p)
     load_rel.wait()
 
     chunks = 2 * ctxw // 128
@@ -419,12 +420,11 @@
 
     for p in range(PAIRS):
         drain_recv(bias_out.at[p, pl.ds(0, GROUP - 1)], b2_recv.at[p])
-    mine = PAIRS * LANES
-    drain_recv(parts_out.at[:, :, pl.ds(0, (GROUP - 1) * mine)], o_recv.at[0])
-    own_part = parts_out.at[:, :, pl.ds(0, mine)]
+    drain_recv(parts_out.at[pl.ds(0, (GROUP - 1) * PAIRS)], o_recv.at[0])
+    own_part = parts_out.at[pl.ds(0, PAIRS)]
     pltpu.make_async_copy(own_part, own_part, o_loc.at[0]).wait()
-    drain_send(parts_out.at[:, :, pl.ds(0, (GROUP - 1) * mine)], o_send.at[0])
-    drain_send(parts_out.at[:, :, pl.ds(0, (GROUP - 1) * mine)], a_send.at[0])
+    drain_send(parts_out.at[pl.ds(0, (GROUP - 1) * PAIRS)], o_send.at[0])
+    drain_send(parts_out.at[pl.ds(0, (GROUP - 1) * PAIRS)], a_send.at[0])
     for direction, exists in ((0, has_lo), (1, has_hi)):
         @pl.when(exists)
         def _():
@@ -437,7 +437,13 @@
 
 def finish(parts, bias, att_out, gq_out, gk_out, gv_out, bias_out, sems):
     outs = (att_out, gq_out, gk_out, gv_out)
-    leave = [pltpu.make_async_copy(parts.at[n], outs[n].at[0], sems.at[n]) for n in range(4)]
+    leave = [
+        pltpu.make_async_copy(
+            parts.at[t, n], outs[n].at[0, :, t * LANES : (t + 1) * LANES], sems.at[n]
+        )
+        for t in range(GROUP * PAIRS)
+        for n in range(4)
+    ]
     for copy in leave:
         copy.start()
     chunks = bias_out.shape[1] // 128
@@ -449,8 +455,8 @@
             place = (chunks - 1 - c) * 128
             bias_out[head : head + 1, place : place + 128] = mirrored[base + c : base + c + 1, :]
         bias_out[head : head + 1, chunks * 128 :] = mirrored[base + chunks : base + chunks + 1, :1]
-    for copy in leave:
-        copy.wait()
+    for n in range(4):
+        pltpu.make_async_copy(outs[n], outs[n], sems.at[n]).wait()
 
 
 def body(queries, keys, values, rel_bias, grad_out):
@@ -473,13 +479,13 @@
     parts, bias = pl.pallas_call(
         functools.partial(kernel, n_dp, n_groups, frames),
         out_shape=(
-            jax.ShapeDtypeStruct((4, frames, width), bf16),
+            jax.ShapeDtypeStruct((GROUP * PAIRS, 4, frames, LANES), bf16),
             jax.ShapeDtypeStruct((PAIRS, GROUP, 16, 128), f32),
         ),
         in_specs=[hbm, hbm, hbm, hbm, hbm],
         out_specs=(anywhere, vmem),
         scratch_shapes=[
-            pltpu.VMEM((4, frames, width), bf16),
+            pltpu.VMEM((GROUP * PAIRS, 4, frames, LANES), bf16),
             pltpu.VMEM(rel_bias.shape, f32),
             pltpu.VMEM((PAIRS, 2, own, LANES), bf16),
             pltpu.VMEM((PAIRS, 2, rows, LANES), bf16),
@@ -500,7 +506,7 @@
             pltpu.VMEM((PAIRS, GROUP, 4, frames, LANES), bf16),
             pltpu.VMEM((PAIRS, n_peer, 16, 128), f32),
             pltpu.VMEM((PAIRS, 16, 128), f32),
-            dma((5,)),
+            dma((2,)),
             dma((1,)),
             dma((PAIRS, GROUP)),
             dma((PAIRS,)),

time: 42.7 us -> 42.4 us (level)
  no operation moved by 1% of the time
where the time goes in v5:
time: 42.4 us; the launch traced here: 42.3 us
  Pallas kernels  41.6 us (98%)
  between operations  0.64 us (2%)
    pallas_call x1, Pallas kernels, body(): pl.pallas_call(functools.partial(kernel, n_dp, n_groups, frames), out_sha...  40 us
    pallas_call x1, Pallas kernels, body(): pl.pallas_call(finish, out_shape=(block, block, block, block, jax.ShapeDt...  1.6 us

profile of v5, /device:TPU:0, one launch (start us, length us, event | category | flops | bytes accessed | tf_op | source)
XLA Modules:
  0.0 42.3 jit_solution(12176448980716663409)
XLA Ops:
  0.6 40.0 %shard_map.92 = (bf16[8,4,128,128]{3,2,1,0:T(8,128)(2,1)S(1)}, f32[2,4,16,128]{3,2,1,0:T(8,128)S(1)}) custom-call(bf16[1,128,1024]{2,1,0:T(8,128)(2,1)} %q_hbm.1, bf16[1,128,1024]{2,1,0:T(8,128)(2,1)} %k_hbm.1, bf16[1,128,1024]{2,1,0:T(8,128)(2,1)} %v_hbm.1, bf16[1,128,1024]{2,1,0:T(8,128)(2,1)} %g_hbm.1, f32[16,769]{1,0:T(8,128)} %rel_hbm.1), custom_call_target="tpu_custom_call" | custom-call | flops 1409286144 | bytes 2097152 | tf_op jit(solution)/shard_map/pallas_call | solution.py:479
  40.7 1.6 %shard_map.93 = (bf16[1,128,1024]{2,1,0:T(8,128)(2,1)}, bf16[1,128,1024]{2,1,0:T(8,128)(2,1)}, bf16[1,128,1024]{2,1,0:T(8,128)(2,1)}, bf16[1,128,1024]{2,1,0:T(8,128)(2,1)}, f32[16,769]{1,0:T(8,128)}) custom-call(bf16[8,4,128,128]{3,2,1,0:T(8,128)(2,1)S(1)} %get-tuple-element.7.parts, f32[2,4,16,128]{3,2,1,0:T(8,128)S(1)} %get-tuple-element.8.bias), custom_call_target="tpu_custom_call" | custom-call | bytes 2097152 | tf_op jit(solution)/shard_map/pallas_call | solution.py:532

commit v6 on v5

--- a/solution.py
+++ b/solution.py
@@ -204,12 +204,12 @@
 
     pl.semaphore_wait(barrier, GROUP - 1 + n_peer - 1)
 
-    def send_inputs(p):
-        for half in range(2):
-            others(lambda j: a_copy(half, p, j).start())
+    def send_inputs(half, p):
+        others(lambda j: a_copy(half, p, j).start())
 
     pltpu.make_async_copy(inbuf, inbuf, loc_sem.at[0]).wait()
-    send_inputs(0)
+    for p in range(PAIRS):
+        send_inputs(0, p)
     for p in range(PAIRS):
         for half in range(2):
             place_own(half, p)
@@ -388,9 +388,9 @@
             send_out(1, p, j)
 
     units = [(p, b) for p in range(PAIRS) for b in ORDER]
-    forward_halo(0)
-    for p in range(1, PAIRS):
-        send_inputs(p)
+    for p in range(PAIRS):
+        forward_halo(p)
+        send_inputs(1, p)
     for n, (p, b) in enumerate(units):
         if b == ORDER[0]:
             wait_inputs(p)
@@ -398,11 +398,8 @@
         if n > 0:
             grad_part(n - 1, *units[n - 1])
             send_grads(*units[n - 1])
-        if b == ORDER[0]:
-            if p + 1 < PAIRS:
-                forward_halo(p + 1)
-            if p > 0:
-                send_bias(p - 1)
+        if b == ORDER[0] and p > 0:
+            send_bias(p - 1)
         if b == ORDER[2] and p > 0:
             sum_bias(p - 1)
             finish_grads(p - 1)

time: 42.4 us -> 41.4 us (0.976)
  Pallas kernels: 41.6 us -> 40.6 us
    pallas_call x1, Pallas kernels: 40 us -> 39 us  [body(): pl.pallas_call(functools.partial(kernel, n_dp, n_groups, frames), out_sha...]
where the time goes in v6:
time: 41.4 us; the launch traced here: 41.2 us
  Pallas kernels  40.6 us (98%)
  between operations  0.64 us (2%)
    pallas_call x1, Pallas kernels, body(): pl.pallas_call(functools.partial(kernel, n_dp, n_groups, frames), out_sha...  39 us
    pallas_call x1, Pallas kernels, body(): pl.pallas_call(finish, out_shape=(block, block, block, block, jax.ShapeDt...  1.6 us

profile of v6, /device:TPU:0, one launch (start us, length us, event | category | flops | bytes accessed | tf_op | source)
XLA Modules:
  0.0 41.2 jit_solution(10550801435332954965)
XLA Ops:
  0.6 39.0 %shard_map.92 = (bf16[8,4,128,128]{3,2,1,0:T(8,128)(2,1)S(1)}, f32[2,4,16,128]{3,2,1,0:T(8,128)S(1)}) custom-call(bf16[1,128,1024]{2,1,0:T(8,128)(2,1)} %q_hbm.1, bf16[1,128,1024]{2,1,0:T(8,128)(2,1)} %k_hbm.1, bf16[1,128,1024]{2,1,0:T(8,128)(2,1)} %v_hbm.1, bf16[1,128,1024]{2,1,0:T(8,128)(2,1)} %g_hbm.1, f32[16,769]{1,0:T(8,128)} %rel_hbm.1), custom_call_target="tpu_custom_call" | custom-call | flops 1409286144 | bytes 2097152 | tf_op jit(solution)/shard_map/pallas_call | solution.py:476
  39.6 1.6 %shard_map.93 = (bf16[1,128,1024]{2,1,0:T(8,128)(2,1)}, bf16[1,128,1024]{2,1,0:T(8,128)(2,1)}, bf16[1,128,1024]{2,1,0:T(8,128)(2,1)}, bf16[1,128,1024]{2,1,0:T(8,128)(2,1)}, f32[16,769]{1,0:T(8,128)}) custom-call(bf16[8,4,128,128]{3,2,1,0:T(8,128)(2,1)S(1)} %get-tuple-element.7.parts, f32[2,4,16,128]{3,2,1,0:T(8,128)S(1)} %get-tuple-element.8.bias), custom_call_target="tpu_custom_call" | custom-call | bytes 2097152 | tf_op jit(solution)/shard_map/pallas_call | solution.py:529
